TPU v7x, 32 devices: a whole 2x2x4 slice. The times are simulated.
32 devices in a mesh: dp: 8 (over z, y), seq: 4 (over x, core).
Axes of the slice: x: 2, y: 2, z: 4, core: 2. Of those that a mesh axis runs over, the one named last changes fastest.
Arguments:
- states: bfloat16 [8, 2560, 768], P('dp', 'seq'), may hold values from -6 to 6
- lengths: int32 [8], P('dp'), may hold values from 640 to 2560, as said below
- teacher: bfloat16 [8, 2560, 768], P('dp', 'seq'), may hold values from -6 to 6
- out_grad: bfloat16 [8, 2560, 768], P('dp', 'seq'), may hold values from -6 to 6
- q_weight: bfloat16 [768, 192], P('dp'), may hold values from -0.4375 to 0.4375
- k_weight: bfloat16 [768, 192], P('dp'), may hold values from -0.4375 to 0.4375
- v_weight: bfloat16 [768, 192], P('dp'), may hold values from -0.4375 to 0.4375
- q_bias: bfloat16 [768], P('dp'), may hold values from -0.59765625 to 0.59765625
- v_bias: bfloat16 [768], P('dp'), may hold values from -0.119628906 to 0.119628906
- o_weight: bfloat16 [768, 768], P('dp'), may hold values from -6 to 6
- o_bias: bfloat16 [768], P('dp'), may hold values from -0.59765625 to 0.59765625
- attn_gain: bfloat16 [768], P('dp'), may hold values from 0.5 to 1.5
- attn_bias: bfloat16 [768], P('dp'), may hold values from -0.59765625 to 0.59765625
- up_weight: bfloat16 [768, 768], P('dp'), may hold values from -0.4375 to 0.4375
- up_bias: bfloat16 [3072], P('dp'), may hold values from -0.59765625 to 0.59765625
- down_weight: bfloat16 [3072, 192], P('dp'), may hold values from -0.21875 to 0.21875
- down_bias: bfloat16 [768], P('dp'), may hold values from -0.59765625 to 0.59765625
- ffn_gain: bfloat16 [768], P('dp'), may hold values from 0.5 to 1.5
- ffn_bias: bfloat16 [768], P('dp'), may hold values from -0.59765625 to 0.59765625
Outputs:
- layer_out: bfloat16 [8, 2560, 768], P('dp', 'seq')
- loss_value: float32 [], replicated
- states_grad: bfloat16 [8, 2560, 768], P('dp', 'seq')
- grad_qw: float32 [768, 192], P('dp')
- grad_kw: float32 [768, 192], P('dp')
- grad_vw: float32 [768, 192], P('dp')
- grad_qb: float32 [768], P('dp')
- grad_vb: float32 [768], P('dp')
- grad_ow: float32 [768, 768], P('dp')
- grad_ob: float32 [768], P('dp')
- grad_ag: float32 [768], P('dp')
- grad_ab: float32 [768], P('dp')
- grad_uw: float32 [768, 768], P('dp')
- grad_ub: float32 [3072], P('dp')
- grad_dw: float32 [3072, 192], P('dp')
- grad_db: float32 [768], P('dp')
- grad_fg: float32 [768], P('dp')
- grad_fb: float32 [768], P('dp')
Inputs may be any that keep to these rules, and one draw needn't show every extreme that they name: `lengths`: every length is an integer from integers from 640 to 2560; some row has exactly 2560 and some other row exactly 640.
All inputs are finite; a program needn't handle non-finite values.
Results may differ from a plain program's by a relative error of at most 0.017.
Values may be sent and summed in bfloat16 or wider, within the bound.
A program may use at most 128 MiB of HBM per device.

v0:
```python
import functools
import math
import types

import jax
import jax.numpy as jnp
from jax import lax
from jax.experimental import pallas as pl
from jax.experimental.pallas import tpu as pltpu
from jax.sharding import PartitionSpec as P

HDIM = 64
GROUPS = 4
EPSILON = 1e-12
NEG_FILL = -1e30
LANES = 128
AUG = 16
LOG2E = 1.4426950408889634
MESH = pl.DeviceIdType.MESH
F32 = jnp.float32
BF16 = jnp.bfloat16
VMEM_LIMIT = 60 * 1024 * 1024


def mm(left, right, left_dim, right_dim):
    return lax.dot_general(
        left, right, (((left_dim,), (right_dim,)), ((), ())), preferred_element_type=F32
    )


def iota(shape, dim):
    return lax.broadcasted_iota(jnp.int32, shape, dim)


def remote(src, dst, send_sem, recv_sem, **where):
    return pltpu.make_async_remote_copy(
        src_ref=src,
        dst_ref=dst,
        send_sem=send_sem,
        recv_sem=recv_sem,
        device_id=where,
        device_id_type=MESH,
    )


def three_parts(row):
    high = row.astype(BF16)
    rest = row - high.astype(F32)
    middle = rest.astype(BF16)
    low = (rest - middle.astype(F32)).astype(BF16)
    return high, middle, low


class Config:
    def __init__(self, dp, seq, piece, width, hidden, shard):
        self.dp, self.seq, self.piece, self.width, self.hidden, self.shard = (
            dp,
            seq,
            piece,
            width,
            hidden,
            shard,
        )
        self.slots = piece * seq
        self.group = width // GROUPS
        self.heads = self.group // HDIM
        self.per_group = dp // GROUPS
        self.split = shard % 32 == 0 and seq == 4 and dp == 8
        self.half = shard // 2
        self.quarter = hidden // dp // 4


def greet(cfg, me, my_dp):
    barrier = pltpu.get_barrier_semaphore()
    count = cfg.seq - 1
    for d in range(1, cfg.seq):
        pl.semaphore_signal(barrier, inc=1, device_id={"seq": me ^ d}, device_id_type=MESH)
    if cfg.split:
        count += cfg.dp - 1
        for e in range(1, cfg.dp):
            pl.semaphore_signal(
                barrier, inc=1, device_id={"dp": lax.rem(my_dp + e, cfg.dp)}, device_id_type=MESH
            )
    return lambda: pl.semaphore_wait(barrier, count)


def layer_kernel(cfg, row, names, *refs):
    r = types.SimpleNamespace(**dict(zip(names, refs, strict=True)))
    split = cfg.split
    me = lax.axis_index("seq")
    my_dp = lax.axis_index("dp")
    piece, width, group, heads, seq = cfg.piece, cfg.width, cfg.group, cfg.heads, cfg.seq
    shard, half, n_dp, per_group = cfg.shard, cfg.half, cfg.dp, cfg.per_group
    hid = cfg.hidden // GROUPS
    n_z = n_dp // 2
    core = lax.rem(me, 2)
    my_z, my_y = my_dp // 2, lax.rem(my_dp, 2)
    far = [d for d in range(seq - 1, 1, -1)]

    states = r.states
    teacher, out_grad = r.states_grad, r.layer_out
    late = [
        pltpu.make_async_copy(r.teacher, teacher, r.late_sem.at[0]),
        pltpu.make_async_copy(r.out_grad, out_grad, r.late_sem.at[1]),
    ]
    x_own, x_group, w_group, w_pad, smalls = (
        r.x_own,
        r.x_group,
        r.w_group,
        r.w_pad,
        r.smalls,
    )
    q_t, k_n, k_t, v_n = r.q_t, r.k_n, r.k_t, r.v_n
    context_s, context_r = r.context_s, r.context_r
    cols, vcols = r.cols, r.vcols
    wide, slim = r.wide, r.slim
    wo, w_up, wd = r.wo, r.w_up, r.wd
    c_grad, d_in, dx_r = r.c_grad, r.d_in, r.dx_r
    dx_s = c_grad
    tall1 = group + AUG
    low = r.low
    low2 = low.at[GROUPS * tall1 :]

    def low1(g, start, size):
        return pl.ds(pl.multiple_of(g * tall1 + start, AUG), size)

    def d_aug(h, t, start, size):
        return pl.ds(pl.multiple_of((h * seq + t) * LANES + start, HDIM), size)

    score0, score1 = wide.at[0:piece], wide.at[piece : 2 * piece]
    gathered = r.gathered
    v1, first, v2, seed = (wide.at[i * width : (i + 1) * width] for i in range(4))
    dq, dk, dv = (wide.at[i * width : (i + 1) * width] for i in range(3))
    act, slope = slim.at[0 : cfg.hidden], slim.at[cfg.hidden : 2 * cfg.hidden]
    p0, p1, s0, s1 = (slim.at[i * piece : (i + 1) * piece] for i in range(4))
    d_t = slope

    def at(i, n):
        return pl.ds(pl.multiple_of(i * n, n), n)

    def loop(count, body, *init):
        return lax.fori_loop(0, count, lambda i, c: body(i, *c), tuple(init))

    def sub(v):
        return jnp.sum(v, axis=0, keepdims=True)


    def to_seq(sems, src, dst, d):
        return remote(src, dst, sems[0].at[d], sems[1].at[d], seq=me ^ d)

    def x_copy(d):
        return to_seq((r.x_send, r.x_recv), x_own.at[at(me ^ d, group)], x_group.at[me, pl.ds(0, group)], d)

    def c_copy(d):
        return to_seq((r.c_send, r.c_recv), context_s.at[me ^ d], context_r.at[at(me, group)], d)

    def g_copy(d):
        return to_seq((r.g_send, r.g_recv), c_grad.at[at(me ^ d, group)], d_in.at[me], d)

    def dx_copy(d):
        return to_seq((r.dx_send, r.dx_recv), dx_s.at[at(me ^ d, group)], dx_r.at[at(me, group)], d)

    if split:
        pack = r.pack
        w_in = r.w_in
        my_slot = lax.rem(my_dp, per_group)
        holder = my_dp // per_group == me

        def s_copy(e):
            return remote(
                smalls.at[my_dp],
                smalls.at[my_dp],
                r.s_send.at[e],
                r.s_recv.at[e],
                dp=lax.rem(my_dp + e, n_dp),
            )

        def w_along(step):
            return remote(
                w_in.at[my_y],
                w_in.at[my_y],
                r.w_send.at[step + 1],
                r.w_recv.at[0],
                dp=my_dp + 2 * step,
            )

        def w_across():
            return remote(
                w_in.at[my_y], w_in.at[my_y], r.w_send.at[1], r.w_recv.at[1], dp=my_dp + 1 - 2 * my_y
            )

        def w_over():
            return remote(
                w_in.at[1 - my_y], w_in.at[1 - my_y], r.w_send.at[1], r.w_recv.at[1], dp=my_dp
            )

        def w_each(fn):
            pl.when((my_z >= me) & (my_z < n_z - 1))(lambda: fn(w_along(1)))
            pl.when((my_z <= me) & (my_z > 0))(lambda: fn(w_along(-1)))
            fn(w_across())

        def hop(kind, i, **where):
            ref = pack.at[i, core]
            return remote(ref, ref, r.hop_send.at[kind, i], r.hop_recv.at[i], **where)

        def up(i):
            return hop(0, i, dp=my_dp + 2)

        def down(i):
            return hop(1, i, dp=my_dp - 2)

        def across(i):
            return hop(2, i, dp=my_dp + 1 - 2 * my_y)

        def beside(i):
            ref = pack.at[i, core]
            return remote(ref, ref, r.sib_send.at[i], r.sib_recv.at[i], seq=me ^ 1)

        def when(condition, fn):
            pl.when(condition)(fn)

        def gather_start():
            when(my_z < n_z - 1, lambda: up(my_dp).start())
            when(my_z > 0, lambda: down(my_dp).start())
            across(my_dp).start()

        def gather_z(k):
            below, above = my_dp - 2 * k, my_dp + 2 * k

            @pl.when(my_z >= k)
            def _():
                hop(0, below, dp=my_dp).wait_recv()
                when(my_z < n_z - 1, lambda: up(below).start())
                across(below).start()
                beside(below).start()

            @pl.when(my_z + k < n_z)
            def _():
                hop(0, above, dp=my_dp).wait_recv()
                when(my_z > 0, lambda: down(above).start())
                across(above).start()
                beside(above).start()

        def gather_y(k):
            other = my_dp + 1 - 2 * my_y

            def take(i):
                hop(2, i, dp=my_dp).wait_recv()
                beside(i).start()

            if k == 0:
                take(other)
            else:
                when(my_z >= k, lambda: take(other - 2 * k))
                when(my_z + k < n_z, lambda: take(other + 2 * k))

        def gather_end():
            for e in range(1, n_dp):
                copy = beside(lax.rem(my_dp + e, n_dp))
                copy.wait()

            when(my_z < n_z - 1, lambda: up(my_dp).wait_send())
            when(my_z > 0, lambda: down(my_dp).wait_send())
            across(my_dp).wait_send()
            for k in range(1, n_z):
                below, above = my_dp - 2 * k, my_dp + 2 * k

                @pl.when(my_z >= k)
                def _():
                    when(my_z < n_z - 1, lambda: up(below).wait_send())
                    across(below).wait_send()

                @pl.when(my_z + k < n_z)
                def _():
                    when(my_z > 0, lambda: down(above).wait_send())
                    across(above).wait_send()


    wait_entry = greet(cfg, me, my_dp)
    for c in range(0, width, LANES):
        x_own[c : c + LANES] = states[:, c : c + LANES].T
    if split:
        for c in range(2):
            pack[my_dp, c, 0] = r.ow[c * half : (c + 1) * half]
            pack[my_dp, c, 1] = r.uw[c * half : (c + 1) * half]
            for k in range(2):
                pack[my_dp, c, 2, :, k * 4 * shard : (k + 1) * 4 * shard] = r.dw[
                    (2 * c + k) * half : (2 * c + k + 1) * half
                ]
        smalls[my_dp] = jnp.zeros((16, LANES), F32)
        for n, ref in enumerate((r.qb, r.vb, r.ob, r.ag, r.ab, r.db, r.fg, r.fb)):
            smalls[my_dp, n : n + 1, 0:shard] = ref[...].astype(F32)
        for n in range(4):
            smalls[my_dp, 8 + n : 9 + n, 0:shard] = r.ub[:, n * shard : (n + 1) * shard].astype(F32)
        for n in range(cfg.rows):
            smalls[my_dp, 12 + n : 13 + n] = jnp.broadcast_to(
                r.lengths[n : n + 1].astype(F32), (1, LANES)
            )

        @pl.when(holder)
        def _():
            w_in[my_y] = jnp.concatenate(
                [ref[...].astype(F32) for ref in (r.wq, r.wk, r.wv)], axis=1
            ).astype(BF16)

    wait_entry()
    if split:
        for e in range(1, n_dp):
            s_copy(e).start()

        @pl.when(holder)
        def _():
            w_each(lambda copy: copy.start())

    for d in range(1, seq):
        x_copy(d).start()
    for copy in late:
        copy.start()
    x_group[me, 0:group] = x_own[at(me, group)]


    n_cols = heads * LANES
    lane = iota((group, n_cols), 1)
    spread = jnp.where(
        (((lane >> 7) * HDIM + (lane & 127)) == iota((group, n_cols), 0)) & ((lane & 127) < HDIM),
        1.0,
        0.0,
    ).astype(BF16)
    if split:
        @pl.when(jnp.logical_not(holder))
        def _():
            remote(
                w_in.at[my_y], w_in.at[my_y], r.w_send.at[1], r.w_recv.at[0], dp=my_dp
            ).wait_recv()
            w_each(lambda copy: copy.start())

        for e in range(1, n_dp):
            s_copy(e).wait_recv()
        w_over().wait_recv()
        for t in range(per_group):
            for kind in range(3):
                w_group[kind, t * shard : (t + 1) * shard] = w_in[
                    t, :, kind * group : (kind + 1) * group
                ]
        gather_start()
    else:
        for kind in range(3):
            w_group[kind] = r.w_all[kind]
    for kind in range(3):
        w_pad[kind, 0:group] = mm(w_group[kind], spread, 1, 0).astype(BF16)
    vec_rows = jnp.zeros((AUG, n_cols), F32)
    lane = iota((LANES, n_cols), 1)
    source = iota((LANES, n_cols), 0)
    for t in range(per_group):
        spread = jnp.where(
            (((lane >> 7) * HDIM + (lane & 127)) == source + t * shard)
            & ((lane & 127) < HDIM)
            & (source < shard),
            1.0,
            0.0,
        ).astype(BF16)
        vec_rows += mm(smalls[me * per_group + t].astype(BF16), spread, 1, 0)
    row_id = iota((AUG, n_cols), 0)
    lane = iota((AUG, n_cols), 1) & 127
    zero = jnp.zeros((AUG, n_cols), F32)
    top_row = row_id == 0
    w_pad[0, group:] = jnp.where(top_row, vec_rows[0:1], zero).astype(BF16)
    ones_k = (top_row & (lane > HDIM) & (lane <= HDIM + 3)) | ((row_id == 1) & (lane == HDIM))
    w_pad[1, group:] = jnp.where(ones_k, 1.0, zero).astype(BF16)
    ones_v = (lane >= HDIM) & (lane < HDIM + 3)
    w_pad[2, group:] = jnp.where(top_row, jnp.where(ones_v, 1.0, vec_rows[1:2]), zero).astype(BF16)

    length = smalls[my_dp, 12 + row : 13 + row, 0:1]
    aug_row = iota((AUG, piece), 0)
    factor = LOG2E * HDIM**-0.5
    deep = HDIM + AUG

    def v_t(h, t):
        return pl.ds(pl.multiple_of((h * seq + t) * deep, AUG), deep)

    def project(t):
        slot = (iota((AUG, piece), 1) + t * piece).astype(F32)
        mask = jnp.where(slot < length, 0.0, NEG_FILL)
        x_group[t, group:] = jnp.where(
            aug_row == 0, 1.0, jnp.where(aug_row == 1, mask, 0.0)
        ).astype(BF16)
        x = x_group[t]
        queries = mm(w_pad[0], x, 0, 0) * factor
        keys_t = mm(w_pad[1], x, 0, 0)
        values_t = mm(w_pad[2], x, 0, 0)
        keys_n = mm(x, w_pad[1], 0, 0)
        values_n = mm(x, w_pad[2], 0, 0)
        rest = jnp.where(iota((HDIM, piece), 0) == 0, 1.0, 0.0).astype(BF16)
        for h in range(heads):
            span = slice(h * LANES, h * LANES + HDIM)
            q_t[h, t, 0:HDIM] = queries[span].astype(BF16)
            q_t[h, t, HDIM:] = rest
            k_t[h, t] = keys_t[span].astype(BF16)
            slim[v_t(h, t)] = values_t[h * LANES : h * LANES + deep].astype(BF16)
            k_n[h, t] = keys_n[:, h * LANES : (h + 1) * LANES].astype(BF16)
            v_n[h, t] = values_n[:, h * LANES : (h + 1) * LANES].astype(BF16)


    tops = r.tops

    def sums(h, t):
        return pl.ds(pl.multiple_of((h * seq + t) * deep, AUG), deep)

    def clear_sums(i, unused):
        gathered[pl.ds(pl.multiple_of(i * deep, AUG), deep)] = jnp.zeros((deep, piece), F32)
        tops[i] = jnp.full((1, piece), NEG_FILL, F32)
        return (unused,)

    loop(heads * seq, clear_sums, 0)

    per_part = seq * heads

    def run(count, place, first_part, last_part, a, b, hooks=()):
        first_part(a, *place(0))

        def two(u, unused):
            if hooks:
                due = u == hooks[0][0]
                for when_u, fn in hooks[1:]:
                    due = due | (u == when_u)

                @pl.when(due)
                def _():
                    for when_u, fn in hooks:
                        pl.when(u == when_u)(fn)

            first_part(b, *place(2 * u + 1))
            last_part(a, *place(2 * u))
            first_part(a, *place(2 * u + 2))
            last_part(b, *place(2 * u + 1))
            return (unused,)

        loop(count // 2 - 1, two, 0)
        first_part(b, *place(count - 1))
        last_part(a, *place(count - 2))
        last_part(b, *place(count - 1))

    def score(buffer, t, h, k):
        buffer[...] = mm(k_n[h, k], q_t[h, t], 1, 0)

    def absorb(buffer, t, h, k):
        i = h * seq + t
        old = tops[i]
        top = jnp.maximum(old, jnp.max(buffer[...], axis=0, keepdims=True))
        weights = jnp.exp2(buffer[...] - top).astype(BF16)
        tops[i] = top
        place = sums(h, t)
        gathered[place] = gathered[place] * jnp.exp2(old - top) + mm(slim[v_t(h, k)], weights, 1, 0)

    def settle(t):
        for h in range(heads):
            total = gathered[sums(h, t)]
            mass = total[HDIM : HDIM + 1]
            context_s[t, h * HDIM : (h + 1) * HDIM] = (total[0:HDIM] / mass).astype(BF16)
            parts = three_parts(-(tops[h * seq + t] + jnp.log2(mass)))
            value = jnp.where(aug_row == 0, 1.0, 0.0)
            for n, part in enumerate(parts):
                value = jnp.where(aug_row == n + 1, part.astype(F32), value)
            q_t[h, t, HDIM:deep] = value.astype(BF16)

    def place_forward(i):
        part, j = i // per_part, lax.rem(i, per_part)
        is_far, tail = lax.rem((part + 1) // 2, 2), part // 3
        d_q = is_far * (4 - part) + (1 - is_far) * (j // (2 * heads))
        h = is_far * (j // seq) + (1 - is_far) * (lax.rem(j, 2 * heads) // 2)
        d_k = is_far * lax.rem(j, seq) + (1 - is_far) * (lax.rem(j, 2) + 2 * tail)
        return me ^ d_q, h, me ^ d_k

    def far_states():
        for d in far:
            x_copy(d).wait_recv()
        loop(2, lambda i, unused: (project(me ^ (2 + i)), unused)[1:], 0)

    def far_context(d):
        settle(me ^ d)
        c_copy(d).start()

    hooks = [
        (per_part // 2 - 1, far_states),
        (per_part, lambda: far_context(far[0])),
        (per_part * 3 // 2, lambda: far_context(far[1])),
    ]
    if split:
        hooks += [
            (6, lambda: gather_z(1)),
            (9, lambda: gather_y(0)),
            (11, lambda: gather_z(2)),
            (13, lambda: gather_y(1)),
            (16, lambda: gather_z(3)),
            (19, lambda: gather_y(2)),
            (22, lambda: gather_y(3)),
        ]
    project(me)
    x_copy(1).wait_recv()
    project(me ^ 1)
    run(4 * per_part, place_forward, score, absorb, score0, score1, hooks)
    settle(me ^ 1)
    c_copy(1).start()
    settle(me)
    context_r[at(me, group)] = context_s[me]
    if split:
        gather_end()

        def unpack(i, unused):
            for c in range(2):
                wo[pl.ds(pl.multiple_of(i * shard + c * half, AUG), half)] = pack[i, c, 0]
                w_up[pl.ds(pl.multiple_of(i * shard + c * half, AUG), half)] = pack[i, c, 1]
                for k in range(2):
                    wd[
                        pl.ds(
                            pl.multiple_of(i // per_group * group + (2 * c + k) * half, AUG), half
                        ),
                        pl.ds(
                            pl.multiple_of(lax.rem(i, per_group) * 4 * shard, LANES), 4 * shard
                        ),
                    ] = pack[i, c, 2, :, k * 4 * shard : (k + 1) * 4 * shard]
            return (unused,)

        loop(n_dp, unpack, 0)


    for i in range(n_dp):
        turned = smalls[i].T
        cols[i * shard : (i + 1) * shard] = turned[0:shard]
    vcols[...] = jnp.zeros_like(vcols)
    inv = 1.0 / width
    total = jnp.sum(smalls[:, 12:13, 0:1], axis=0)
    for n in range(1, cfg.rows):
        total += jnp.sum(smalls[:, 12 + n : 13 + n, 0:1], axis=0)
    slot = (iota((1, piece), 1) + me * piece).astype(F32)
    live = jnp.where(slot < length, 1.0, 0.0)
    coef = 2.0 / (total * width)
    zero_row = jnp.zeros((1, piece), F32)

    def col(i, n, which):
        return cols[at(i, n), which : which + 1]

    for d in range(1, seq):
        c_copy(d).wait_recv()

    step = 256

    def attn_out(i, acc):
        out = mm(wo[:, at(i, step)], context_r[...], 0, 0)
        v = out + x_own[at(i, step)].astype(F32) + col(i, step, 2)
        v1[at(i, step)] = v
        return (acc + sub(v),)

    (acc,) = loop(width // step, attn_out, zero_row)
    mean = acc * inv

    def center(ref):
        def body(g, acc):
            v = ref[at(g, group)] - mean
            ref[at(g, group)] = v
            return (acc + sub(v * v),)

        (acc,) = loop(GROUPS, body, zero_row)
        return lax.rsqrt(acc * inv + EPSILON)

    scale1 = center(v1)

    def norm1(g, unused):
        v = v1[at(g, group)] * scale1
        v1[at(g, group)] = v
        out = v * col(g, group, 3) + col(g, group, 4)
        first[at(g, group)] = out
        low[low1(g, 0, group)] = out.astype(BF16)
        low[low1(g, group, AUG)] = jnp.where(aug_row == 0, 1.0, 0.0).astype(BF16)
        return (unused,)

    loop(GROUPS, norm1, 0)

    def gelu(u):
        d = 1.0 + (0.3275911 * 0.7071067811865476) * jnp.abs(u)
        t = pl.reciprocal(d, approx=True)
        t = t * (2.0 - d * t)
        bell = jnp.exp2((u * u) * (-0.5 * LOG2E))
        poly = t * (
            0.127414796
            + t * (-0.142248368 + t * (0.7107068705 + t * (-0.7265760135 + t * 0.5307027145)))
        )
        tail = poly * bell
        phi = jnp.where(u >= 0.0, 1.0 - tail, tail)
        return u * phi, phi + u * bell * 0.3989422804014327

    bunch = max(1, LANES // math.gcd(LANES, 4 * shard) if (4 * shard) % LANES else 1)
    span4 = 4 * shard * bunch
    n_steps = n_dp // bunch
    steps_group = n_steps // GROUPS
    tall = span4 // 4

    raw0, raw1 = wide.at[2 * width : 2 * width + span4], wide.at[3 * width : 3 * width + span4]

    def expand(raw, i):
        g, c = i // steps_group, lax.rem(i, steps_group)
        raw[...] = mm(w_up[at(g, group), at(c, span4)], low[low1(g, 0, group)], 0, 0)

    def activate(raw, i):
        bias = jnp.concatenate(
            [cols[at(i * bunch + n, shard), 8 + b : 9 + b] for n in range(bunch) for b in range(4)],
            axis=0,
        )
        for b in range(4):
            part = slice(b * tall, (b + 1) * tall)
            out, grad = gelu(raw[part] + bias[part])
            place = pl.ds(pl.multiple_of((i * 4 + b) * tall, tall), tall)
            act[place] = out.astype(BF16)
            slope[place] = grad.astype(BF16)

    run(n_steps, lambda i: (i,), expand, activate, raw0, raw1)

    def contract(g, acc):
        out = mm(wd[at(g, group)], act[at(g, hid)], 1, 0)
        v = out + first[at(g, group)] + col(g, group, 5)
        v2[at(g, group)] = v
        return (acc + sub(v),)

    (acc,) = loop(GROUPS, contract, zero_row)
    mean = acc * inv
    scale2 = center(v2)

    for copy in late:
        copy.wait()
    loss, sum1, sum2 = zero_row, zero_row, zero_row
    for c in range(width // LANES):
        span = slice(c * LANES, (c + 1) * LANES)
        xhat = v2[span] * scale2
        v2[span] = xhat
        gain = cols[span, 6:7]
        full = xhat * gain + cols[span, 7:8]
        error = full - teacher[:, span].T.astype(F32)
        loss += sub(live * error * error)
        grad = live * (out_grad[:, span].T.astype(F32) + error * coef)
        r.layer_out[:, span] = full.astype(BF16).T
        vcols[span, 4:5] = jnp.sum(grad * xhat, axis=1, keepdims=True)
        vcols[span, 5:6] = jnp.sum(grad, axis=1, keepdims=True)
        grad = grad * gain
        seed[span] = grad
        sum1 += sub(grad)
        sum2 += sub(grad * xhat)
    sum1, sum2 = sum1 * inv, sum2 * inv

    def back2(g, unused):
        place = at(g, group)
        grad = scale2 * (seed[place] - sum1 - v2[place] * sum2)
        seed[place] = grad
        brief = grad.astype(BF16)
        low2[place] = brief
        vcols[place, 3:4] = jnp.sum(brief.astype(F32), axis=1, keepdims=True)
        return (unused,)

    loop(GROUPS, back2, 0)

    def back_act(i, unused):
        place = at(i, span4)
        g, c = i // steps_group, lax.rem(i, steps_group)
        raw = mm(wd[at(g, group), at(c, span4)], low2[at(g, group)], 0, 0)
        slope[place] = (raw * slope[place].astype(F32)).astype(BF16)
        return (unused,)

    loop(n_steps, back_act, 0)

    def back_first(g, a, b):
        place = at(g, group)
        grad = seed[place] + mm(w_up[place], slope[at(g, hid)], 1, 0)
        xhat = v1[place]
        vcols[place, 1:2] = jnp.sum(grad * xhat, axis=1, keepdims=True)
        vcols[place, 2:3] = jnp.sum(grad, axis=1, keepdims=True)
        grad = grad * col(g, group, 3)
        seed[place] = grad
        return (a + sub(grad), b + sub(grad * xhat))


    vecs = r.vecs
    if split:
        other_y = my_dp + 1 - 2 * my_y
        side, cross, spread_z, spread_v = r.side, r.cross, r.spread_z, r.spread_v
        od_out, vec_out = r.od_out, r.vec_out
        red_send, red_recv = r.red_send, r.red_recv

        def side_copies():
            return (
                remote(
                    pack.at[:, 1 - core, pl.ds(1, 2)],
                    side.at[:, pl.ds(1, 2)],
                    red_send.at[0],
                    red_recv.at[0],
                    seq=me ^ 1,
                ),
                remote(
                    pack.at[:, 1 - core, 0],
                    side.at[:, 0],
                    red_send.at[6],
                    red_recv.at[6],
                    seq=me ^ 1,
                ),
                remote(vecs, r.vec_side, red_send.at[1], red_recv.at[1], seq=me ^ 1),
            )

        def cross_copy(j):
            z = lax.rem(my_z + 1 + j, n_z)
            return remote(
                side.at[2 * z + 1 - my_y],
                cross.at[z],
                r.cross_send.at[z],
                r.cross_recv.at[z],
                dp=other_y,
            )

        def vec_cross():
            return remote(
                r.vec_mine, r.vec_cross, red_send.at[2], red_recv.at[2], dp=other_y
            )

        def z_copy(j):
            z = lax.rem(my_z + 1 + j, n_z)
            return remote(
                side.at[2 * z + my_y],
                spread_z.at[my_z],
                r.z_send.at[j],
                r.z_recv.at[j],
                dp=2 * z + my_y,
            )

        def vz_copy(j):
            z = lax.rem(my_z + 1 + j, n_z)
            return remote(
                r.vec_sum,
                spread_v.at[my_z],
                r.vz_send.at[j],
                r.vz_recv.at[j],
                dp=2 * z + my_y,
            )

        def x_copies():
            return (
                remote(
                    r.x_mine, r.x_theirs, red_send.at[3], red_recv.at[3], seq=me ^ 2
                ),
                remote(r.vec_z, r.vec_x, red_send.at[4], red_recv.at[4], seq=me ^ 2),
            )

        def last_copy():
            return remote(
                od_out.at[core], od_out.at[core], red_send.at[5], red_recv.at[5], seq=me ^ 1
            )

        def reduce_side():
            for copy in side_copies():
                copy.wait_recv()

            def add(i, unused):
                side[i] = (pack[i, core].astype(F32) + side[i].astype(F32)).astype(BF16)
                return (unused,)

            loop(n_dp, add, 0)
            r.vec_mine[...] = vecs[...] + r.vec_side[...]
            vec_cross().start()
            for j in range(n_z):
                cross_copy(j).start()

        def reduce_cross(j):
            cross_copy(j).wait_recv()
            z = lax.rem(my_z + 1 + j, n_z)
            i = 2 * z + my_y
            side[i] = (side[i].astype(F32) + cross[z].astype(F32)).astype(BF16)
            if j < n_z - 1:
                z_copy(j).start()

        def reduce_vec():
            vec_cross().wait_recv()
            value = r.vec_mine[...] + r.vec_cross[...]
            r.vec_sum[...] = value
            spread_v[my_z] = value
            for j in range(n_z - 1):
                vz_copy(j).start()

        def reduce_z():
            for j in range(n_z - 1):
                z_copy(j).wait_recv()
                vz_copy(j).wait_recv()
            spread_z[my_z] = side[my_dp]
            value = spread_z[0].astype(F32)
            vec = spread_v[0]
            for z in range(1, n_z):
                value += spread_z[z].astype(F32)
                vec += spread_v[z]
            r.x_mine[...] = value.astype(BF16)
            r.vec_z[...] = vec
            for copy in x_copies():
                copy.start()

        def reduce_x():
            for copy in x_copies():
                copy.wait_recv()
            od_out[core] = r.x_mine[...].astype(F32) + r.x_theirs[...].astype(F32)
            vec_out[...] = r.vec_z[...] + r.vec_x[...]
            last_copy().start()

    vecs[...] = jnp.zeros_like(vecs)
    for g in range(GROUPS):
        out = mm(low[low1(g, 0, tall1)], slope[g * hid : (g + 1) * hid], 1, 1)
        vecs[8 + g : 9 + g] = out[group : group + 1]
        if split:
            for t in range(per_group):
                for c in range(2):
                    base = shard * t + half * c
                    pack[g * per_group + t, c, 1] = out[base : base + half].astype(BF16)
        else:
            r.g_all[1, g * group : (g + 1) * group] = out[0:group].astype(BF16)
    sum1, sum2 = loop(GROUPS, back_first, zero_row, zero_row)
    sum1, sum2 = sum1 * inv, sum2 * inv

    for g in range(GROUPS):
        out = mm(low2[g * group : (g + 1) * group], act[g * hid : (g + 1) * hid], 1, 1)
        if split:
            for t in range(per_group):
                for c in range(2):
                    for k in range(2):
                        pack[g * per_group + t, c, 2, :, k * 4 * shard : (k + 1) * 4 * shard] = (
                            out[
                                (2 * c + k) * half : (2 * c + k + 1) * half,
                                t * 4 * shard : (t + 1) * 4 * shard,
                            ].astype(BF16)
                        )
        else:
            r.g_all[2, g * group : (g + 1) * group] = out.astype(BF16)

    if split:
        side_copies()[0].start()

    def back1(g, unused):
        place = at(g, group)
        grad = scale1 * (seed[place] - sum1 - v1[place] * sum2)
        seed[place] = grad
        brief = grad.astype(BF16)
        low2[place] = brief
        vcols[place, 0:1] = jnp.sum(brief.astype(F32), axis=1, keepdims=True)
        return (unused,)

    loop(GROUPS, back1, 0)
    grad_mid = seed

    def back_context(i, unused):
        c_grad[at(i, step)] = mm(wo[at(i, step)], low2[...], 1, 0).astype(BF16)
        return (unused,)

    loop(width // step, back_context, 0)
    for d in [1] + far:
        g_copy(d).start()

    vecs[0:8] = vcols[...].T[0:8]
    mean_loss = jnp.sum(loss, axis=1, keepdims=True) / (total * width)
    vecs[12:13] = jnp.broadcast_to(mean_loss, (1, width))
    for j in range(2):
        rows = width // 2
        out = mm(context_r[j * rows : (j + 1) * rows], low2[...], 1, 1)
        if split:
            for t in range(n_dp // 2):
                for c in range(2):
                    base = shard * t + half * c
                    pack[j * (n_dp // 2) + t, c, 0] = out[base : base + half].astype(BF16)
        else:
            r.g_all[0, j * rows : (j + 1) * rows] = out.astype(BF16)

    if split:
        for copy in side_copies()[1:]:
            copy.start()


    def clear(i, unused):
        for ref in (dq, dk, dv):
            ref[at(i, HDIM)] = jnp.zeros((HDIM, piece), F32)
        return (unused,)

    loop(heads * seq, clear, 0)
    tail_row = iota((HDIM, piece), 0)

    def prepare(t):
        for h in range(heads):
            span = slice(h * HDIM, (h + 1) * HDIM)
            grad = d_in[t, span]
            low[d_aug(h, t, 0, HDIM)] = grad
            parts = three_parts(-sub(grad.astype(F32) * context_s[t, span].astype(F32)))
            value = jnp.zeros((HDIM, piece), F32)
            for n, part in enumerate(parts):
                value = jnp.where(tail_row == n, part.astype(F32), value)
            low[d_aug(h, t, HDIM, HDIM)] = value.astype(BF16)

    def rows_of(h, t):
        return at(h * seq + t, HDIM)

    def weigh(buffers, t, h, k):
        p, s = buffers
        weights = jnp.exp2(mm(q_t[h, t], k_n[h, k], 0, 1))
        p[...] = weights.astype(BF16)
        s[...] = (weights * mm(low[d_aug(h, t, 0, LANES)], v_n[h, k], 0, 1)).astype(BF16)

    def gather_grads(buffers, t, h, k):
        p, s = buffers
        dv[rows_of(h, k)] += mm(low[d_aug(h, t, 0, HDIM)], p[...], 1, 0)
        dk[rows_of(h, k)] += mm(q_t[h, t, 0:HDIM], s[...], 1, 0)
        dq[rows_of(h, t)] += mm(k_t[h, k], s[...], 1, 1)

    def turned(t, kind, h):
        return pl.ds(pl.multiple_of((t * 3 + kind) * group + h * HDIM, HDIM), HDIM)

    def fill(t, h):
        for kind, (ref, scale) in enumerate(((dq, HDIM**-0.5), (dk, 1.0 / LOG2E), (dv, 1.0))):
            d_t[turned(t, kind, h)] = (ref[rows_of(h, t)] * scale).astype(BF16)

    def whole(t, kind):
        return pl.ds(pl.multiple_of((t * 3 + kind) * group, HDIM), group)

    def states_part(t):
        out = mm(w_group[0], d_t[whole(t, 0)], 1, 0)
        out += mm(w_group[1], d_t[whole(t, 1)], 1, 0)
        out += mm(w_group[2], d_t[whole(t, 2)], 1, 0)
        dx_s[at(t, group)] = out.astype(BF16)

    if split:
        qkv_s, qkv_r, qkv_out = r.qkv_s, r.qkv_r, r.qkv_out
        owner = my_dp // per_group == me

        def qkv_copy(h, t):
            return remote(
                qkv_s.at[h, t],
                qkv_r.at[h, my_dp],
                r.q1_send.at[h, t],
                r.q1_recv.at[h, my_dp],
                dp=me * per_group + t,
            )

        def qkv_share(h, d):
            return remote(
                qkv_out.at[h], qkv_out.at[h], r.q2_send.at[h, d], r.q2_recv.at[h], seq=me ^ d
            )

    def emit(h):
        for d in range(2):
            fill(me ^ d, h)
        totals = []
        for kind in range(3):
            value = mm(x_group[0], d_t[turned(0, kind, h)], 1, 1)
            for t in range(1, seq):
                value += mm(x_group[t], d_t[turned(t, kind, h)], 1, 1)
            totals.append(value)
        if split:
            bias_rows = jnp.zeros((shard, HDIM), F32)
            bias_id = iota((shard, HDIM), 0)
            for kind in range(3):
                bias_rows = jnp.where(bias_id == kind, totals[kind][group : group + 1], bias_rows)
            for t in range(per_group):
                qkv_s[h, t] = jnp.concatenate(
                    [value[t * shard : (t + 1) * shard] for value in totals] + [bias_rows], axis=1
                ).astype(BF16)
                when(me * per_group + t != my_dp, lambda: qkv_copy(h, t).start())
        else:
            for kind in range(3):
                r.qkv_raw[h, kind] = totals[kind]

    def place_backward(i):
        part, j = i // per_part, lax.rem(i, per_part)
        is_far, tail = lax.rem((part + 1) // 2, 2), part // 3
        near = 1 - is_far
        d_q = is_far * (4 - part) + near * (
            (1 - tail) * (j // (2 * heads)) + tail * (lax.rem(j, 4) // 2)
        )
        h = is_far * (j // seq) + near * (
            (1 - tail) * (lax.rem(j, 2 * heads) // 2) + tail * (j // 4)
        )
        d_k = is_far * lax.rem(j, seq) + near * (lax.rem(j, 2) + 2 * (1 - tail))
        return me ^ d_q, h, me ^ d_k

    def receive(d):
        g_copy(d).wait_recv()
        prepare(me ^ d)

    def far_states_grads():
        for d in range(1, seq):
            g_copy(d).wait_send()
        for d in far:
            for h in range(heads):
                fill(me ^ d, h)
            states_part(me ^ d)
            dx_copy(d).start()

    hooks = [
        (heads - 1, lambda: receive(1)),
        (per_part // 2 - 1, lambda: receive(far[0])),
        (per_part - 1, lambda: receive(far[1])),
        (per_part * 3 // 2, far_states_grads),
        (per_part * 3 // 2 + 2, lambda: emit(0)),
        (per_part * 3 // 2 + 4, lambda: emit(1)),
    ]
    if split:
        hooks += [
            (1, reduce_side),
            (4, lambda: reduce_cross(0)),
            (7, lambda: reduce_cross(1)),
            (8, reduce_vec),
            (10, lambda: reduce_cross(2)),
            (13, lambda: reduce_cross(3)),
            (19, reduce_z),
        ]
    d_in[me] = c_grad[at(me, group)]
    prepare(me)
    run(4 * per_part, place_backward, weigh, gather_grads, (p0, s0), (p1, s1), hooks)
    emit(2)
    states_part(me ^ 1)
    dx_copy(1).start()
    states_part(me)
    dx_r[at(me, group)] = dx_s[at(me, group)]
    if split:
        reduce_x()

        @pl.when(owner)
        def _():
            for h in range(heads):
                value = qkv_s[h, my_slot].astype(F32)
                for e in range(1, n_dp):
                    src = lax.rem(my_dp + e, n_dp)
                    remote(
                        qkv_s.at[h, 0],
                        qkv_r.at[h, src],
                        r.q1_send.at[h, 0],
                        r.q1_recv.at[h, src],
                        dp=src,
                    ).wait_recv()
                    value += qkv_r[h, src].astype(F32)
                qkv_out[h] = value.astype(BF16)
                for d in range(1, seq):
                    qkv_share(h, d).start()

    for d in range(1, seq):
        dx_copy(d).wait_recv()
    for c in range(width // LANES):
        span = slice(c * LANES, (c + 1) * LANES)
        r.states_grad[:, span] = (dx_r[span].astype(F32) + grad_mid[span]).astype(BF16).T


    for d in range(1, seq):
        x_copy(d).wait_send()
        c_copy(d).wait_send()
        dx_copy(d).wait_send()
    if split:
        last_copy().wait()
        for h in range(heads):
            for t in range(per_group):
                when(me * per_group + t != my_dp, lambda: qkv_copy(h, t).wait_send())

        @pl.when(owner)
        def _():
            for h in range(heads):
                for d in range(1, seq):
                    qkv_share(h, d).wait_send()

        @pl.when(jnp.logical_not(owner))
        def _():
            for h in range(heads):
                qkv_share(h, 1).wait_recv()

        for e in range(1, n_dp):
            s_copy(e).wait_send()

        w_each(lambda copy: copy.wait_send())
        for copy in side_copies() + x_copies():
            copy.wait_send()
        vec_cross().wait_send()
        for j in range(n_z):
            cross_copy(j).wait_send()
        for j in range(n_z - 1):
            z_copy(j).wait_send()
            vz_copy(j).wait_send()


def layer(cfg, row, collective_id, inputs):
    c = cfg
    g, l, h, s, w, f = c.group, c.piece, c.heads, c.seq, c.width, c.hidden
    n_z = c.dp // 2
    sds = jax.ShapeDtypeStruct
    dma = pltpu.SemaphoreType.DMA
    vm = pltpu.VMEM
    outputs = dict(layer_out=sds((l, w), BF16), states_grad=sds((l, w), BF16))
    if c.split:
        outputs |= dict(
            od_out=sds((2, 3, c.half, w), F32),
            qkv_out=sds((h, c.shard, 4 * HDIM), BF16),
            vec_out=sds((16, w), F32),
        )
    else:
        outputs |= dict(
            g_all=sds((3, w, w), BF16),
            qkv_raw=sds((h, 3, g + AUG, HDIM), F32),
            vecs=sds((16, w), F32),
        )
    scratch = dict(
        x_own=vm((w, l), BF16),
        x_group=vm((s, g + AUG, l), BF16),
        w_group=vm((3, g, g), BF16),
        w_pad=vm((3, g + AUG, h * LANES), BF16),
        q_t=vm((h, s, LANES, l), BF16),
        k_n=vm((h, s, l, LANES), BF16),
        k_t=vm((h, s, HDIM, l), BF16),
        v_n=vm((h, s, l, LANES), BF16),
        context_s=vm((s, g, l), BF16),
        context_r=vm((w, l), BF16),
        tops=vm((h * s, 1, l), F32),
        gathered=vm((h * s * (HDIM + AUG), l), F32),
        cols=vm((w, 16), F32),
        vcols=vm((w, LANES), F32),
        wide=vm((4 * w, l), F32),
        slim=vm((2 * f, l), BF16),
        c_grad=vm((w, l), BF16),
        d_in=vm((s, g, l), BF16),
        dx_r=vm((w, l), BF16),
        low=vm((GROUPS * (g + AUG) + w, l), BF16),
        late_sem=dma((2,)),
        x_send=dma((s,)),
        x_recv=dma((s,)),
        c_send=dma((s,)),
        c_recv=dma((s,)),
        g_send=dma((s,)),
        g_recv=dma((s,)),
        dx_send=dma((s,)),
        dx_recv=dma((s,)),
    )
    if c.split:
        unit = (3, c.half, w)
        vec = (16, w)
        scratch |= dict(
            wo=vm((w, w), BF16),
            w_up=vm((w, w), BF16),
            wd=vm((w, f // GROUPS), BF16),
            smalls=vm((c.dp, 16, LANES), F32),
            pack=vm((c.dp, 2) + unit, BF16),
            w_in=vm((c.per_group, c.shard, 3 * g), BF16),
            vecs=vm(vec, F32),
            side=vm((c.dp,) + unit, BF16),
            cross=vm((n_z,) + unit, BF16),
            spread_z=vm((n_z,) + unit, BF16),
            spread_v=vm((n_z,) + vec, F32),
            x_mine=vm(unit, BF16),
            x_theirs=vm(unit, BF16),
            vec_side=vm(vec, F32),
            vec_mine=vm(vec, F32),
            vec_cross=vm(vec, F32),
            vec_sum=vm(vec, F32),
            vec_z=vm(vec, F32),
            vec_x=vm(vec, F32),
            qkv_s=vm((h, c.per_group, c.shard, 4 * HDIM), BF16),
            qkv_r=vm((h, c.dp, c.shard, 4 * HDIM), BF16),
            s_send=dma((c.dp,)),
            s_recv=dma((c.dp,)),
            w_send=dma((3,)),
            w_recv=dma((2,)),
            hop_send=dma((3, c.dp)),
            hop_recv=dma((c.dp,)),
            sib_send=dma((c.dp,)),
            sib_recv=dma((c.dp,)),
            red_send=dma((7,)),
            red_recv=dma((7,)),
            cross_send=dma((n_z,)),
            cross_recv=dma((n_z,)),
            z_send=dma((n_z,)),
            z_recv=dma((n_z,)),
            vz_send=dma((n_z,)),
            vz_recv=dma((n_z,)),
            q1_send=dma((h, c.per_group)),
            q1_recv=dma((h, c.dp)),
            q2_send=dma((h, s)),
            q2_recv=dma((h,)),
        )
    names = tuple(inputs) + tuple(outputs) + tuple(scratch)
    vmem = pl.BlockSpec(memory_space=pltpu.VMEM)
    results = pl.pallas_call(
        functools.partial(layer_kernel, cfg, row, names),
        out_shape=list(outputs.values()),
        in_specs=[
            pl.BlockSpec(memory_space=pl.ANY) if v is inputs["teacher"] or v is inputs["out_grad"] else vmem
            for v in inputs.values()
        ],
        out_specs=[vmem] * len(outputs),
        scratch_shapes=list(scratch.values()),
        compiler_params=pltpu.CompilerParams(
            collective_id=collective_id, has_side_effects=True, vmem_limit_bytes=VMEM_LIMIT
        ),
        name="layer",
    )(*inputs.values())
    return dict(zip(outputs, results, strict=True))


def deliver_kernel(cfg, layer_in, states_in, qkv, od, vec, *outs):
    my_dp = lax.axis_index("dp")
    shard, width, group, half = cfg.shard, cfg.width, cfg.group, cfg.half
    layer_out, states_grad, qw, kw, vw, ow, uw, dw = outs[:8]
    layer_out[...] = layer_in[...]
    states_grad[...] = states_in[...]
    parts = [
        jnp.concatenate(
            [qkv[h, :, k * HDIM : (k + 1) * HDIM].astype(F32) for h in range(cfg.heads)], axis=1
        )
        for k in range(4)
    ]
    for ref, part in zip((qw, kw, vw), parts[:3], strict=True):
        ref[...] = part
    for c in range(2):
        rows = slice(c * half, (c + 1) * half)
        ow[rows] = od[c, 0]
        uw[rows] = od[c, 1]
        for k in range(2):
            dw[(2 * c + k) * half : (2 * c + k + 1) * half] = od[
                c, 2, :, k * 4 * shard : (k + 1) * 4 * shard
            ]
    slot = lax.rem(my_dp, cfg.per_group)
    mine = parts[3][0:8, 0:shard]
    for t in range(1, cfg.per_group):
        mine = jnp.where(slot == t, parts[3][0:8, t * shard : (t + 1) * shard], mine)
    outs[8][...] = mine[0:1]
    outs[9][...] = mine[2:3]
    turned = pltpu.roll(vec[0:8], lax.rem(width - my_dp * shard, width), 1)
    for n in range(6):
        outs[10 + n][...] = turned[n : n + 1, 0:shard]
    outs[16][...] = vec[
        pl.ds(8 + my_dp // cfg.per_group, 1),
        pl.ds(pl.multiple_of(slot * 4 * shard, LANES), 4 * shard),
    ]
    outs[17][...] = vec[12:13, 0:1]


def deliver(cfg, *args):
    sds = jax.ShapeDtypeStruct
    shard, width, group = cfg.shard, cfg.width, cfg.group
    out_shape = [sds(a.shape, a.dtype) for a in args[:2]]
    out_shape += [sds((shard, group), F32)] * 3 + [sds((shard, width), F32)] * 2
    out_shape += [sds((group, 4 * shard), F32)] + [sds((1, shard), F32)] * 8
    out_shape += [sds((1, 4 * shard), F32), sds((1, 1), F32)]
    vmem = pl.BlockSpec(memory_space=pltpu.VMEM)
    return pl.pallas_call(
        functools.partial(deliver_kernel, cfg),
        out_shape=out_shape,
        in_specs=[vmem] * len(args),
        out_specs=[vmem] * len(out_shape),
        name="deliver",
    )(*args)


def local(
    states,
    lengths,
    teacher,
    out_grad,
    q_weight,
    k_weight,
    v_weight,
    q_bias,
    v_bias,
    o_weight,
    o_bias,
    attn_gain,
    attn_bias,
    up_weight,
    up_bias,
    down_weight,
    down_bias,
    ffn_gain,
    ffn_bias,
):
    row_count, piece, width = states.shape
    n_dp, n_seq = lax.axis_size("dp"), lax.axis_size("seq")
    me, my_dp = lax.axis_index("seq"), lax.axis_index("dp")
    shard = q_bias.shape[0]
    hidden = up_bias.shape[0] * n_dp
    cfg = Config(n_dp, n_seq, piece, width, hidden, shard)
    cfg.rows = row_count
    group = cfg.group

    if not cfg.split:

        def pad(v):
            return jnp.pad(v.astype(F32), ((0, 0), (0, LANES - v.shape[1])))

        vectors = (q_bias, v_bias, o_bias, attn_gain, attn_bias, down_bias, ffn_gain, ffn_bias)
        small = jnp.concatenate(
            [
                pad(jnp.stack(vectors)),
                pad(up_bias.reshape(4, shard)),
                jnp.broadcast_to(lengths.astype(F32)[:, None], (row_count, LANES)),
                jnp.zeros((4 - row_count, LANES), F32),
            ]
        )
        smalls = lax.all_gather(small, "dp", axis=0)
        qkv = jnp.stack((q_weight, k_weight, v_weight))
        qkv = lax.all_gather(qkv, "dp", axis=1, tiled=True)
        w_group_in = lax.dynamic_slice(qkv, (0, me * group, 0), (3, group, group))
        wo = lax.all_gather(o_weight, "dp", axis=0, tiled=True)
        wu = lax.all_gather(up_weight, "dp", axis=0, tiled=True)
        wd = lax.all_gather(down_weight, "dp", axis=0, tiled=True)
        wd = wd.reshape(GROUPS, -1, group).transpose(0, 2, 1).reshape(width, -1)

    results = []
    for n in range(row_count):
        inputs = dict(states=states[n], teacher=teacher[n], out_grad=out_grad[n])
        if cfg.split:
            inputs |= dict(
                wq=q_weight,
                wk=k_weight,
                wv=v_weight,
                ow=o_weight,
                uw=up_weight,
                dw=down_weight.T,
                qb=q_bias[None],
                vb=v_bias[None],
                ob=o_bias[None],
                ag=attn_gain[None],
                ab=attn_bias[None],
                db=down_bias[None],
                fg=ffn_gain[None],
                fb=ffn_bias[None],
                ub=up_bias[None],
                lengths=lengths[:, None],
            )
        else:
            inputs |= dict(smalls=smalls, w_all=w_group_in, wo=wo, w_up=wu, wd=wd)
        results.append(layer(cfg, n, n, inputs))

    def summed(name):
        first = results[0][name]
        if row_count == 1:
            return first
        return sum((item[name].astype(F32) for item in results[1:]), first.astype(F32))

    if cfg.split:
        heavy = [jnp.stack([item[n] for item in results]) for n in ("layer_out", "states_grad")]
        out = deliver(cfg, *heavy, summed("qkv_out"), summed("od_out"), summed("vec_out"))
        grad_qw, grad_kw, grad_vw, grad_ow, grad_uw, grad_dw = out[2:8]
        vectors = [v[0] for v in out[8:17]]
        return (
            (out[0], out[17][0, 0], out[1], grad_qw, grad_kw, grad_vw)
            + (vectors[0], vectors[1], grad_ow, *vectors[2:5], grad_uw, vectors[8])
            + (grad_dw.T, *vectors[5:8])
        )

    layer_out = jnp.stack([item["layer_out"] for item in results])
    states_grad = jnp.stack([item["states_grad"] for item in results])
    qkv_g, g_all, vecs = (summed(n).astype(F32) for n in ("qkv_raw", "g_all", "vecs"))
    qkv_g = qkv_g.transpose(1, 2, 0, 3).reshape(3, group + AUG, group)
    whole = jnp.zeros((3, width + GROUPS * AUG, group), F32)
    whole = lax.dynamic_update_slice(whole, qkv_g[:, :group], (0, me * group, 0))
    whole = lax.dynamic_update_slice(whole, qkv_g[:, group:], (0, width + me * AUG, 0))
    whole, g_all, vec = lax.psum((whole, g_all, vecs), ("dp", "seq"))
    qkv = lax.dynamic_slice(whole, (0, my_dp * shard, 0), (3, shard, group))
    biases = whole[:, width::AUG].reshape(3, width)
    grad_qb = lax.dynamic_slice(biases[0], (my_dp * shard,), (shard,))
    grad_vb = lax.dynamic_slice(biases[2], (my_dp * shard,), (shard,))
    g_ou = lax.dynamic_slice(g_all[:2], (0, my_dp * shard, 0), (2, shard, width))
    g_d = g_all[2].reshape(GROUPS, group, -1).transpose(0, 2, 1).reshape(-1, group)
    grad_dw = lax.dynamic_slice(g_d, (my_dp * 4 * shard, 0), (4 * shard, group))
    mine = lax.dynamic_slice(vec[:6], (0, my_dp * shard), (6, shard))
    grad_ub = lax.dynamic_slice(vec[8:12].reshape(-1), (my_dp * 4 * shard,), (4 * shard,))
    return (
        (layer_out, vec[12, 0], states_grad, qkv[0], qkv[1], qkv[2], grad_qb, grad_vb, g_ou[0])
        + (mine[0], mine[1], mine[2], g_ou[1], grad_ub, grad_dw, mine[3], mine[4], mine[5])
    )


def solution(mesh):
    rows3 = P("dp", "seq", None)
    matrix = P("dp", None)
    vector = P("dp")
    return jax.shard_map(
        local,
        mesh=mesh,
        in_specs=(rows3, vector, rows3, rows3)
        + (matrix,) * 3
        + (vector,) * 2
        + (matrix,)
        + (vector,) * 3
        + (matrix, vector, matrix)
        + (vector,) * 3,
        out_specs=(rows3, P(), rows3)
        + (matrix,) * 3
        + (vector,) * 2
        + (matrix,)
        + (vector,) * 3
        + (matrix, vector, matrix)
        + (vector,) * 3,
        check_vma=False,
    )
```

profile of v0, /device:TPU:0, one launch (start us, length us, event | category | flops | bytes accessed | tf_op | source)
XLA Modules:
  0.0 161.5 jit_solution(10893315372271821717)
XLA Ops:
  1.3 0.0 copy-start.1
  1.3 0.7 copy-done.1
  2.0 0.6 broadcast_in_dim.38.refs_17_
  2.5 154.0 %layer.1 = (bf16[640,768]{1,0:T(8,128)(2,1)}, bf16[640,768]{1,0:T(8,128)(2,1)}, f32[2,3,48,768]{3,2,1,0:T(8,128)}, bf16[3,96,256]{2,1,0:T(8,128)(2,1)}, f32[16,768]{1,0:T(8,128)}) custom-call(bf16[640,768]{1,0:T(8,128)(2,1)} %bitcast.28, bf16[640,768]{1,0:T(8,128)(2,1)} %bitcast.29, bf16[640,768]{1,0:T(8,128)(2,1)} %bitcast.30, bf16[96,192]{1,0:T(8,128)(2,1)} %refs_3_.1, ...), custom_call_target="tpu_custom_call" | custom-call | tf_op jit(solution)/shard_map/layer/pallas_call | solution.py:1182
  156.5 3.6 %deliver.1 = (bf16[1,640,768]{2,1,0:T(8,128)(2,1)}, bf16[1,640,768]{2,1,0:T(8,128)(2,1)}, f32[96,192]{1,0:T(8,128)}, f32[96,192]{1,0:T(8,128)}, f32[96,192]{1,0:...) custom-call(bf16[1,640,768]{2,1,0:T(8,128)(2,1)} %bitcast.26, ...), custom_call_target="tpu_custom_call" | custom-call | tf_op jit(solution)/shard_map/deliver/pallas_call | solution.py:1245
  160.2 0.0 copy-start
  160.2 0.7 copy-done
  160.9 0.6 reduce
Async XLA Ops:
  1.3 0.7 copy-start.1
  160.2 0.7 copy-start
where the time goes:
time: 162 us; the launch traced here: 161 us
  Pallas kernels  158 us (98%)
  local copies, waits for them, and re-layouts  1.91 us (1%)
    pallas_call x1, Pallas kernels, layer(): pl.pallas_call(functools.partial(layer_kernel, cfg, row, names), out_shap...  154 us
    pallas_call x1, Pallas kernels, deliver(): pl.pallas_call(functools.partial(deliver_kernel, cfg), out_shape=out_shap...  3.64 us

commit v1 on v0

--- a/solution.py
+++ b/solution.py
@@ -164,7 +164,6 @@
         pack = r.pack
         w_in = r.w_in
         my_slot = lax.rem(my_dp, per_group)
-        holder = my_dp // per_group == me
 
         def s_copy(e):
             return remote(
@@ -175,29 +174,32 @@
                 dp=lax.rem(my_dp + e, n_dp),
             )
 
-        def w_along(step):
+        first_group = me - core
+
+        def w_ref(g):
+            return w_in.at[g, my_y, core]
+
+        def w_along(g, j):
+            z = lax.rem(my_z + n_z - 1 - j, n_z)
             return remote(
-                w_in.at[my_y],
-                w_in.at[my_y],
-                r.w_send.at[step + 1],
-                r.w_recv.at[0],
-                dp=my_dp + 2 * step,
+                w_ref(g), w_ref(g), r.w_send.at[g, j], r.w_recv.at[g, 0], dp=2 * z + my_y
             )
 
-        def w_across():
+        def w_across(g):
             return remote(
-                w_in.at[my_y], w_in.at[my_y], r.w_send.at[1], r.w_recv.at[1], dp=my_dp + 1 - 2 * my_y
+                w_ref(g), w_ref(g), r.w_send.at[g, n_z], r.w_recv.at[g, 1], dp=my_dp + 1 - 2 * my_y
             )
 
-        def w_over():
-            return remote(
-                w_in.at[1 - my_y], w_in.at[1 - my_y], r.w_send.at[1], r.w_recv.at[1], dp=my_dp
-            )
-
-        def w_each(fn):
-            pl.when((my_z >= me) & (my_z < n_z - 1))(lambda: fn(w_along(1)))
-            pl.when((my_z <= me) & (my_z > 0))(lambda: fn(w_along(-1)))
-            fn(w_across())
+        def w_over(g):
+            ref = w_in.at[g, 1 - my_y, core]
+            return remote(ref, ref, r.w_send.at[g, n_z], r.w_recv.at[g, 1], dp=my_dp)
+
+        def w_beside(g, part, half_of):
+            ref = w_in.at[g, my_y if part == 0 else 1 - my_y, half_of]
+            return remote(ref, ref, r.wb_send.at[part], r.wb_recv.at[part], seq=me ^ 1)
+
+        def holds(g):
+            return my_z == first_group + g
 
         def hop(kind, i, **where):
             ref = pack.at[i, core]
@@ -289,31 +291,40 @@
                 ]
         smalls[my_dp] = jnp.zeros((16, LANES), F32)
         for n, ref in enumerate((r.qb, r.vb, r.ob, r.ag, r.ab, r.db, r.fg, r.fb)):
-            smalls[my_dp, n : n + 1, 0:shard] = ref[...].astype(F32)
+            smalls[my_dp, n : n + 1, 0:shard] = ref[...].reshape(1, shard).astype(F32)
+        up_bias = r.ub[...].reshape(1, 4 * shard).astype(F32)
         for n in range(4):
-            smalls[my_dp, 8 + n : 9 + n, 0:shard] = r.ub[:, n * shard : (n + 1) * shard].astype(F32)
+            smalls[my_dp, 8 + n : 9 + n, 0:shard] = up_bias[:, n * shard : (n + 1) * shard]
         for n in range(cfg.rows):
-            smalls[my_dp, 12 + n : 13 + n] = jnp.broadcast_to(
-                r.lengths[n : n + 1].astype(F32), (1, LANES)
-            )
-
-        @pl.when(holder)
-        def _():
-            w_in[my_y] = jnp.concatenate(
-                [ref[...].astype(F32) for ref in (r.wq, r.wk, r.wv)], axis=1
-            ).astype(BF16)
+            smalls[my_dp, 12 + n : 13 + n] = jnp.full((1, LANES), r.lengths[n].astype(F32))
+
+        for g in range(2):
+
+            @pl.when(holds(g))
+            def _():
+                for c in range(2):
+                    rows = slice(c * half, (c + 1) * half)
+                    w_in[g, my_y, c] = jnp.concatenate(
+                        [ref[rows].astype(F32) for ref in (r.wq, r.wk, r.wv)], axis=1
+                    ).astype(BF16)
 
     wait_entry()
     if split:
         for e in range(1, n_dp):
             s_copy(e).start()
 
-        @pl.when(holder)
-        def _():
-            w_each(lambda copy: copy.start())
+        for g in range(2):
+
+            @pl.when(holds(g))
+            def _():
+                for j in range(n_z - 1):
+                    w_along(g, j).start()
+                w_across(g).start()
 
     for d in range(1, seq):
         x_copy(d).start()
+    if split:
+        gather_start()
     for copy in late:
         copy.start()
     x_group[me, 0:group] = x_own[at(me, group)]
@@ -327,22 +338,29 @@
         0.0,
     ).astype(BF16)
     if split:
-        @pl.when(jnp.logical_not(holder))
-        def _():
-            remote(
-                w_in.at[my_y], w_in.at[my_y], r.w_send.at[1], r.w_recv.at[0], dp=my_dp
-            ).wait_recv()
-            w_each(lambda copy: copy.start())
-
+        for n, g in enumerate((1 - core, core)):
+
+            @pl.when(jnp.logical_not(holds(g)))
+            def _():
+                w_along(g, 0).wait_recv()
+                w_across(g).start()
+                if n == 0:
+                    w_beside(g, 0, core).start()
+
+        for n, g in enumerate((1 - core, core)):
+            w_over(g).wait_recv()
+            if n == 0:
+                w_beside(g, 1, core).start()
         for e in range(1, n_dp):
             s_copy(e).wait_recv()
-        w_over().wait_recv()
+        when(my_z != me, lambda: w_beside(core, 0, 1 - core).wait_recv())
+        w_beside(core, 1, 1 - core).wait_recv()
         for t in range(per_group):
-            for kind in range(3):
-                w_group[kind, t * shard : (t + 1) * shard] = w_in[
-                    t, :, kind * group : (kind + 1) * group
-                ]
-        gather_start()
+            for c in range(2):
+                for kind in range(3):
+                    w_group[kind, t * shard + c * half : t * shard + (c + 1) * half] = w_in[
+                        core, t, c, :, kind * group : (kind + 1) * group
+                    ]
     else:
         for kind in range(3):
             w_group[kind] = r.w_all[kind]
@@ -487,13 +505,13 @@
     ]
     if split:
         hooks += [
-            (6, lambda: gather_z(1)),
-            (9, lambda: gather_y(0)),
-            (11, lambda: gather_z(2)),
-            (13, lambda: gather_y(1)),
-            (16, lambda: gather_z(3)),
-            (19, lambda: gather_y(2)),
-            (22, lambda: gather_y(3)),
+            (2, lambda: gather_z(1)),
+            (6, lambda: gather_y(0)),
+            (8, lambda: gather_z(2)),
+            (11, lambda: gather_y(1)),
+            (13, lambda: gather_z(3)),
+            (16, lambda: gather_y(2)),
+            (20, lambda: gather_y(3)),
         ]
     project(me)
     x_copy(1).wait_recv()
@@ -578,8 +596,7 @@
 
     def gelu(u):
         d = 1.0 + (0.3275911 * 0.7071067811865476) * jnp.abs(u)
-        t = pl.reciprocal(d, approx=True)
-        t = t * (2.0 - d * t)
+        t = pltpu.reciprocal(d, approx=True)
         bell = jnp.exp2((u * u) * (-0.5 * LOG2E))
         poly = t * (
             0.127414796
@@ -1002,7 +1019,7 @@
     if split:
         hooks += [
             (1, reduce_side),
-            (4, lambda: reduce_cross(0)),
+            (5, lambda: reduce_cross(0)),
             (7, lambda: reduce_cross(1)),
             (8, reduce_vec),
             (10, lambda: reduce_cross(2)),
@@ -1069,7 +1086,20 @@
         for e in range(1, n_dp):
             s_copy(e).wait_send()
 
-        w_each(lambda copy: copy.wait_send())
+        for g in range(2):
+
+            @pl.when(holds(g))
+            def _():
+                for j in range(n_z - 1):
+                    w_along(g, j).wait_send()
+
+            w_across(g).wait_send()
+
+            @pl.when(core != g)
+            def _():
+                when(jnp.logical_not(holds(g)), lambda: w_beside(g, 0, core).wait_send())
+                w_beside(g, 1, core).wait_send()
+
         for copy in side_copies() + x_copies():
             copy.wait_send()
         vec_cross().wait_send()
@@ -1140,7 +1170,7 @@
             wd=vm((w, f // GROUPS), BF16),
             smalls=vm((c.dp, 16, LANES), F32),
             pack=vm((c.dp, 2) + unit, BF16),
-            w_in=vm((c.per_group, c.shard, 3 * g), BF16),
+            w_in=vm((2, c.per_group, 2, c.half, 3 * g), BF16),
             vecs=vm(vec, F32),
             side=vm((c.dp,) + unit, BF16),
             cross=vm((n_z,) + unit, BF16),
@@ -1158,8 +1188,10 @@
             qkv_r=vm((h, c.dp, c.shard, 4 * HDIM), BF16),
             s_send=dma((c.dp,)),
             s_recv=dma((c.dp,)),
-            w_send=dma((3,)),
-            w_recv=dma((2,)),
+            w_send=dma((2, n_z + 1)),
+            w_recv=dma((2, 2)),
+            wb_send=dma((2,)),
+            wb_recv=dma((2,)),
             hop_send=dma((3, c.dp)),
             hop_recv=dma((c.dp,)),
             sib_send=dma((c.dp,)),
@@ -1179,13 +1211,12 @@
         )
     names = tuple(inputs) + tuple(outputs) + tuple(scratch)
     vmem = pl.BlockSpec(memory_space=pltpu.VMEM)
+    hbm = pl.BlockSpec(memory_space=pl.ANY)
+    special = dict(teacher=hbm, out_grad=hbm, lengths=pl.BlockSpec(memory_space=pltpu.SMEM))
     results = pl.pallas_call(
         functools.partial(layer_kernel, cfg, row, names),
         out_shape=list(outputs.values()),
-        in_specs=[
-            pl.BlockSpec(memory_space=pl.ANY) if v is inputs["teacher"] or v is inputs["out_grad"] else vmem
-            for v in inputs.values()
-        ],
+        in_specs=[special.get(name, vmem) for name in inputs],
         out_specs=[vmem] * len(outputs),
         scratch_shapes=list(scratch.values()),
         compiler_params=pltpu.CompilerParams(
@@ -1196,12 +1227,13 @@
     return dict(zip(outputs, results, strict=True))
 
 
-def deliver_kernel(cfg, layer_in, states_in, qkv, od, vec, *outs):
+def deliver_kernel(cfg, layer_in, states_in, qkv, od, vec, *refs):
+    outs = refs
     my_dp = lax.axis_index("dp")
-    shard, width, group, half = cfg.shard, cfg.width, cfg.group, cfg.half
-    layer_out, states_grad, qw, kw, vw, ow, uw, dw = outs[:8]
-    layer_out[...] = layer_in[...]
-    states_grad[...] = states_in[...]
+    shard, width, half = cfg.shard, cfg.width, cfg.half
+    outs[0][...] = layer_in[...]
+    outs[1][...] = states_in[...]
+    qw, kw, vw, ow, uw, dw = outs[2:8]
     parts = [
         jnp.concatenate(
             [qkv[h, :, k * HDIM : (k + 1) * HDIM].astype(F32) for h in range(cfg.heads)], axis=1
@@ -1222,16 +1254,16 @@
     mine = parts[3][0:8, 0:shard]
     for t in range(1, cfg.per_group):
         mine = jnp.where(slot == t, parts[3][0:8, t * shard : (t + 1) * shard], mine)
-    outs[8][...] = mine[0:1]
-    outs[9][...] = mine[2:3]
+    outs[8][...] = mine[0]
+    outs[9][...] = mine[2]
     turned = pltpu.roll(vec[0:8], lax.rem(width - my_dp * shard, width), 1)
     for n in range(6):
-        outs[10 + n][...] = turned[n : n + 1, 0:shard]
+        outs[10 + n][...] = turned[n, 0:shard]
     outs[16][...] = vec[
         pl.ds(8 + my_dp // cfg.per_group, 1),
         pl.ds(pl.multiple_of(slot * 4 * shard, LANES), 4 * shard),
-    ]
-    outs[17][...] = vec[12:13, 0:1]
+    ][0]
+    outs[17][0] = vec[12, 0]
 
 
 def deliver(cfg, *args):
@@ -1239,14 +1271,14 @@
     shard, width, group = cfg.shard, cfg.width, cfg.group
     out_shape = [sds(a.shape, a.dtype) for a in args[:2]]
     out_shape += [sds((shard, group), F32)] * 3 + [sds((shard, width), F32)] * 2
-    out_shape += [sds((group, 4 * shard), F32)] + [sds((1, shard), F32)] * 8
-    out_shape += [sds((1, 4 * shard), F32), sds((1, 1), F32)]
+    out_shape += [sds((group, 4 * shard), F32)] + [sds((shard,), F32)] * 8
+    out_shape += [sds((4 * shard,), F32), sds((1,), F32)]
     vmem = pl.BlockSpec(memory_space=pltpu.VMEM)
     return pl.pallas_call(
         functools.partial(deliver_kernel, cfg),
         out_shape=out_shape,
         in_specs=[vmem] * len(args),
-        out_specs=[vmem] * len(out_shape),
+        out_specs=[vmem] * (len(out_shape) - 1) + [pl.BlockSpec(memory_space=pltpu.SMEM)],
         name="deliver",
     )(*args)
 
@@ -1315,16 +1347,16 @@
                 ow=o_weight,
                 uw=up_weight,
                 dw=down_weight.T,
-                qb=q_bias[None],
-                vb=v_bias[None],
-                ob=o_bias[None],
-                ag=attn_gain[None],
-                ab=attn_bias[None],
-                db=down_bias[None],
-                fg=ffn_gain[None],
-                fb=ffn_bias[None],
-                ub=up_bias[None],
-                lengths=lengths[:, None],
+                qb=q_bias,
+                vb=v_bias,
+                ob=o_bias,
+                ag=attn_gain,
+                ab=attn_bias,
+                db=down_bias,
+                fg=ffn_gain,
+                fb=ffn_bias,
+                ub=up_bias,
+                lengths=lengths,
             )
         else:
             inputs |= dict(smalls=smalls, w_all=w_group_in, wo=wo, w_up=wu, wd=wd)
@@ -1340,9 +1372,9 @@
         heavy = [jnp.stack([item[n] for item in results]) for n in ("layer_out", "states_grad")]
         out = deliver(cfg, *heavy, summed("qkv_out"), summed("od_out"), summed("vec_out"))
         grad_qw, grad_kw, grad_vw, grad_ow, grad_uw, grad_dw = out[2:8]
-        vectors = [v[0] for v in out[8:17]]
+        vectors = out[8:17]
         return (
-            (out[0], out[17][0, 0], out[1], grad_qw, grad_kw, grad_vw)
+            (out[0], out[17].reshape(()), out[1], grad_qw, grad_kw, grad_vw)
             + (vectors[0], vectors[1], grad_ow, *vectors[2:5], grad_uw, vectors[8])
             + (grad_dw.T, *vectors[5:8])
         )

time: 162 us -> 156 us (0.963)
  Pallas kernels: 158 us -> 154 us
  local copies, waits for them, and re-layouts: 1.91 us -> 0 us
    pallas_call x1, Pallas kernels: 154 us -> 150 us  [layer(): pl.pallas_call(functools.partial(layer_kernel, cfg, row, names), out_shap...]
where the time goes in v1:
time: 156 us; the launch traced here: 155 us
  Pallas kernels  154 us (99%)
    pallas_call x1, Pallas kernels, layer(): pl.pallas_call(functools.partial(layer_kernel, cfg, row, names), out_shap...  150 us
    pallas_call x1, Pallas kernels, deliver(): pl.pallas_call(functools.partial(deliver_kernel, cfg), out_shape=out_shap...  3.65 us

profile of v1, /device:TPU:0, one launch (start us, length us, event | category | flops | bytes accessed | tf_op | source)
XLA Modules:
  0.0 155.0 jit_solution(9344819054159010027)
XLA Ops:
  1.3 149.9 %layer.1 = (bf16[640,768]{1,0:T(8,128)(2,1)}, bf16[640,768]{1,0:T(8,128)(2,1)}, f32[2,3,48,768]{3,2,1,0:T(8,128)}, bf16[3,96,256]{2,1,0:T(8,128)(2,1)}, f32[16,768]{1,0:T(8,128)}) custom-call(bf16[640,768]{1,0:T(8,128)(2,1)} %bitcast.8, bf16[640,768]{1,0:T(8,128)(2,1)} %bitcast.9, bf16[640,768]{1,0:T(8,128)(2,1)} %bitcast.10, bf16[96,192]{1,0:T(8,128)(2,1)} %refs_3_.1, ...), custom_call_target="tpu_custom_call" | custom-call | tf_op jit(solution)/shard_map/layer/pallas_call | solution.py:1216
  151.2 3.6 %deliver.1 = (bf16[1,640,768]{2,1,0:T(8,128)(2,1)}, bf16[1,640,768]{2,1,0:T(8,128)(2,1)}, f32[96,192]{1,0:T(8,128)}, f32[96,192]{1,0:T(8,128)}, f32[96,192]{1,0:...) custom-call(bf16[1,640,768]{2,1,0:T(8,128)(2,1)} %bitcast.11, ...), custom_call_target="tpu_custom_call" | custom-call | tf_op jit(solution)/shard_map/deliver/pallas_call | solution.py:1277

commit v2 on v1

--- a/solution.py
+++ b/solution.py
@@ -224,7 +224,6 @@
         def gather_start():
             when(my_z < n_z - 1, lambda: up(my_dp).start())
             when(my_z > 0, lambda: down(my_dp).start())
-            across(my_dp).start()
 
         def gather_z(k):
             below, above = my_dp - 2 * k, my_dp + 2 * k
@@ -323,20 +322,24 @@
 
     for d in range(1, seq):
         x_copy(d).start()
-    if split:
-        gather_start()
     for copy in late:
         copy.start()
     x_group[me, 0:group] = x_own[at(me, group)]
 
 
+    deep = HDIM + AUG
+    tops = r.tops
+
+    def sums(h, t):
+        return pl.ds(pl.multiple_of((h * seq + t) * deep, AUG), deep)
+
+    def clear_sums(i, unused):
+        gathered[pl.ds(pl.multiple_of(i * deep, AUG), deep)] = jnp.zeros((deep, piece), F32)
+        tops[i] = jnp.full((1, piece), NEG_FILL, F32)
+        return (unused,)
+
+    loop(heads * seq, clear_sums, 0)
     n_cols = heads * LANES
-    lane = iota((group, n_cols), 1)
-    spread = jnp.where(
-        (((lane >> 7) * HDIM + (lane & 127)) == iota((group, n_cols), 0)) & ((lane & 127) < HDIM),
-        1.0,
-        0.0,
-    ).astype(BF16)
     if split:
         for n, g in enumerate((1 - core, core)):
 
@@ -347,25 +350,12 @@
                 if n == 0:
                     w_beside(g, 0, core).start()
 
-        for n, g in enumerate((1 - core, core)):
-            w_over(g).wait_recv()
-            if n == 0:
-                w_beside(g, 1, core).start()
+        gather_start()
         for e in range(1, n_dp):
             s_copy(e).wait_recv()
-        when(my_z != me, lambda: w_beside(core, 0, 1 - core).wait_recv())
-        w_beside(core, 1, 1 - core).wait_recv()
-        for t in range(per_group):
-            for c in range(2):
-                for kind in range(3):
-                    w_group[kind, t * shard + c * half : t * shard + (c + 1) * half] = w_in[
-                        core, t, c, :, kind * group : (kind + 1) * group
-                    ]
-    else:
-        for kind in range(3):
-            w_group[kind] = r.w_all[kind]
-    for kind in range(3):
-        w_pad[kind, 0:group] = mm(w_group[kind], spread, 1, 0).astype(BF16)
+    for i in range(n_dp):
+        turned_small = smalls[i].T
+        cols[i * shard : (i + 1) * shard] = turned_small[0:shard]
     vec_rows = jnp.zeros((AUG, n_cols), F32)
     lane = iota((LANES, n_cols), 1)
     source = iota((LANES, n_cols), 0)
@@ -388,11 +378,35 @@
     ones_v = (lane >= HDIM) & (lane < HDIM + 3)
     w_pad[2, group:] = jnp.where(top_row, jnp.where(ones_v, 1.0, vec_rows[1:2]), zero).astype(BF16)
 
+    if split:
+        for n, g in enumerate((1 - core, core)):
+            w_over(g).wait_recv()
+            if n == 0:
+                w_beside(g, 1, core).start()
+        across(my_dp).start()
+        when(my_z != me, lambda: w_beside(core, 0, 1 - core).wait_recv())
+        w_beside(core, 1, 1 - core).wait_recv()
+        for t in range(per_group):
+            for c in range(2):
+                for kind in range(3):
+                    w_group[kind, t * shard + c * half : t * shard + (c + 1) * half] = w_in[
+                        core, t, c, :, kind * group : (kind + 1) * group
+                    ]
+    else:
+        for kind in range(3):
+            w_group[kind] = r.w_all[kind]
+    lane = iota((group, n_cols), 1)
+    spread = jnp.where(
+        (((lane >> 7) * HDIM + (lane & 127)) == iota((group, n_cols), 0)) & ((lane & 127) < HDIM),
+        1.0,
+        0.0,
+    ).astype(BF16)
+    for kind in range(3):
+        w_pad[kind, 0:group] = mm(w_group[kind], spread, 1, 0).astype(BF16)
+
     length = smalls[my_dp, 12 + row : 13 + row, 0:1]
     aug_row = iota((AUG, piece), 0)
     factor = LOG2E * HDIM**-0.5
-    deep = HDIM + AUG
-
     def v_t(h, t):
         return pl.ds(pl.multiple_of((h * seq + t) * deep, AUG), deep)
 
@@ -419,24 +433,13 @@
             v_n[h, t] = values_n[:, h * LANES : (h + 1) * LANES].astype(BF16)
 
 
-    tops = r.tops
-
-    def sums(h, t):
-        return pl.ds(pl.multiple_of((h * seq + t) * deep, AUG), deep)
-
-    def clear_sums(i, unused):
-        gathered[pl.ds(pl.multiple_of(i * deep, AUG), deep)] = jnp.zeros((deep, piece), F32)
-        tops[i] = jnp.full((1, piece), NEG_FILL, F32)
-        return (unused,)
-
-    loop(heads * seq, clear_sums, 0)
-
     per_part = seq * heads
 
-    def run(count, place, first_part, last_part, a, b, hooks=()):
+    def run(count, place, first_part, last_part, a, b, hooks=(), rest=None, unroll=2):
+        buffers = (a, b)
         first_part(a, *place(0))
 
-        def two(u, unused):
+        def several(u, unused):
             if hooks:
                 due = u == hooks[0][0]
                 for when_u, fn in hooks[1:]:
@@ -447,16 +450,27 @@
                     for when_u, fn in hooks:
                         pl.when(u == when_u)(fn)
 
-            first_part(b, *place(2 * u + 1))
-            last_part(a, *place(2 * u))
-            first_part(a, *place(2 * u + 2))
-            last_part(b, *place(2 * u + 1))
+            for j in range(unroll):
+                first_part(buffers[(j + 1) % 2], *place(unroll * u + j + 1))
+                last_part(buffers[j % 2], *place(unroll * u + j))
             return (unused,)
 
-        loop(count // 2 - 1, two, 0)
-        first_part(b, *place(count - 1))
-        last_part(a, *place(count - 2))
-        last_part(b, *place(count - 1))
+        turns = (count - 1) // unroll
+        loop(turns, several, 0)
+        if rest is not None:
+            rest()
+        for i in range(turns * unroll, count - 1):
+            first_part(buffers[(i + 1) % 2], *place(i + 1))
+            last_part(buffers[i % 2], *place(i))
+        last_part(buffers[(count - 1) % 2], *place(count - 1))
+
+    unroll = 4
+
+    def before(step):
+        return (step - 1) // unroll
+
+    def after(step):
+        return step // unroll + 1
 
     def score(buffer, t, h, k):
         buffer[...] = mm(k_n[h, k], q_t[h, t], 1, 0)
@@ -499,24 +513,24 @@
         c_copy(d).start()
 
     hooks = [
-        (per_part // 2 - 1, far_states),
-        (per_part, lambda: far_context(far[0])),
-        (per_part * 3 // 2, lambda: far_context(far[1])),
+        (before(per_part), far_states),
+        (after(2 * per_part - 1), lambda: far_context(far[0])),
+        (after(3 * per_part - 1), lambda: far_context(far[1])),
     ]
     if split:
         hooks += [
-            (2, lambda: gather_z(1)),
-            (6, lambda: gather_y(0)),
-            (8, lambda: gather_z(2)),
-            (11, lambda: gather_y(1)),
-            (13, lambda: gather_z(3)),
-            (16, lambda: gather_y(2)),
-            (20, lambda: gather_y(3)),
+            (1, lambda: gather_z(1)),
+            (3, lambda: gather_y(0)),
+            (4, lambda: gather_z(2)),
+            (6, lambda: gather_y(1)),
+            (7, lambda: gather_z(3)),
+            (8, lambda: gather_y(2)),
+            (10, lambda: gather_y(3)),
         ]
     project(me)
     x_copy(1).wait_recv()
     project(me ^ 1)
-    run(4 * per_part, place_forward, score, absorb, score0, score1, hooks)
+    run(4 * per_part, place_forward, score, absorb, score0, score1, hooks, unroll=unroll)
     settle(me ^ 1)
     c_copy(1).start()
     settle(me)
@@ -542,9 +556,6 @@
         loop(n_dp, unpack, 0)
 
 
-    for i in range(n_dp):
-        turned = smalls[i].T
-        cols[i * shard : (i + 1) * shard] = turned[0:shard]
     vcols[...] = jnp.zeros_like(vcols)
     inv = 1.0 / width
     total = jnp.sum(smalls[:, 12:13, 0:1], axis=0)
@@ -982,17 +993,27 @@
             for kind in range(3):
                 r.qkv_raw[h, kind] = totals[kind]
 
+    early = 2 * (2 * heads + 2)
+    shift = 2 * per_part - early
+
     def place_backward(i):
-        part, j = i // per_part, lax.rem(i, per_part)
-        is_far, tail = lax.rem((part + 1) // 2, 2), part // 3
-        near = 1 - is_far
-        d_q = is_far * (4 - part) + near * (
-            (1 - tail) * (j // (2 * heads)) + tail * (lax.rem(j, 4) // 2)
+        part, m = (i + shift) // (2 * per_part), lax.rem(i + shift, 2 * per_part)
+        is_far, tail = lax.rem(part, 2), part // 2
+        start = (1 - is_far) * (1 - tail)
+        j = lax.rem(i, early // 2)
+        own = j // (2 * heads)
+        n = lax.rem(m, per_part)
+        d_q = (
+            start * (i // (early // 2))
+            + is_far * (seq - 1 - m // per_part)
+            + tail * (lax.rem(m, 4) // 2)
         )
-        h = is_far * (j // seq) + near * (
-            (1 - tail) * (lax.rem(j, 2 * heads) // 2) + tail * (j // 4)
+        h = start * (1 - own) * (j // 2) + is_far * (n // seq) + tail * (1 + m // 4)
+        d_k = (
+            start * ((1 - own) * (2 + lax.rem(j, 2)) + own * (j - 2 * heads))
+            + is_far * lax.rem(m, seq)
+            + tail * lax.rem(m, 2)
         )
-        d_k = is_far * lax.rem(j, seq) + near * (lax.rem(j, 2) + 2 * (1 - tail))
         return me ^ d_q, h, me ^ d_k
 
     def receive(d):
@@ -1008,27 +1029,37 @@
             states_part(me ^ d)
             dx_copy(d).start()
 
+    far_done = after(early + 2 * per_part - 1)
     hooks = [
-        (heads - 1, lambda: receive(1)),
-        (per_part // 2 - 1, lambda: receive(far[0])),
-        (per_part - 1, lambda: receive(far[1])),
-        (per_part * 3 // 2, far_states_grads),
-        (per_part * 3 // 2 + 2, lambda: emit(0)),
-        (per_part * 3 // 2 + 4, lambda: emit(1)),
+        (before(early // 2), lambda: receive(1)),
+        (before(early), lambda: receive(far[0])),
+        (before(early + per_part), lambda: receive(far[1])),
+        (far_done, far_states_grads),
+        (far_done, lambda: emit(0)),
     ]
     if split:
         hooks += [
             (1, reduce_side),
-            (5, lambda: reduce_cross(0)),
-            (7, lambda: reduce_cross(1)),
-            (8, reduce_vec),
-            (10, lambda: reduce_cross(2)),
-            (13, lambda: reduce_cross(3)),
-            (19, reduce_z),
+            (3, lambda: reduce_cross(0)),
+            (3, reduce_vec),
+            (4, lambda: reduce_cross(1)),
+            (5, lambda: reduce_cross(2)),
+            (7, lambda: reduce_cross(3)),
+            (10, reduce_z),
         ]
     d_in[me] = c_grad[at(me, group)]
     prepare(me)
-    run(4 * per_part, place_backward, weigh, gather_grads, (p0, s0), (p1, s1), hooks)
+    run(
+        4 * per_part,
+        place_backward,
+        weigh,
+        gather_grads,
+        (p0, s0),
+        (p1, s1),
+        hooks,
+        lambda: emit(1),
+        unroll,
+    )
     emit(2)
     states_part(me ^ 1)
     dx_copy(1).start()

time: 156 us -> 152 us (0.974)
  Pallas kernels: 154 us -> 150 us
    pallas_call x1, Pallas kernels: 150 us -> 146 us  [layer(): pl.pallas_call(functools.partial(layer_kernel, cfg, row, names), out_shap...]
where the time goes in v2:
time: 152 us
  Pallas kernels  150 us (99%)
    pallas_call x1, Pallas kernels, layer(): pl.pallas_call(functools.partial(layer_kernel, cfg, row, names), out_shap...  146 us
    pallas_call x1, Pallas kernels, deliver(): pl.pallas_call(functools.partial(deliver_kernel, cfg), out_shape=out_shap...  3.65 us

profile of v2, /device:TPU:0, one launch (start us, length us, event | category | flops | bytes accessed | tf_op | source)
XLA Modules:
  0.0 151.5 jit_solution(9251387784394944562)
XLA Ops:
  1.3 146.4 %layer.1 = (bf16[640,768]{1,0:T(8,128)(2,1)}, bf16[640,768]{1,0:T(8,128)(2,1)}, f32[2,3,48,768]{3,2,1,0:T(8,128)}, bf16[3,96,256]{2,1,0:T(8,128)(2,1)}, f32[16,768]{1,0:T(8,128)}) custom-call(bf16[640,768]{1,0:T(8,128)(2,1)} %bitcast.8, bf16[640,768]{1,0:T(8,128)(2,1)} %bitcast.9, bf16[640,768]{1,0:T(8,128)(2,1)} %bitcast.10, bf16[96,192]{1,0:T(8,128)(2,1)} %refs_3_.1, ...), custom_call_target="tpu_custom_call" | custom-call | tf_op jit(solution)/shard_map/layer/pallas_call | solution.py:1247
  147.7 3.6 %deliver.1 = (bf16[1,640,768]{2,1,0:T(8,128)(2,1)}, bf16[1,640,768]{2,1,0:T(8,128)(2,1)}, f32[96,192]{1,0:T(8,128)}, f32[96,192]{1,0:T(8,128)}, f32[96,192]{1,0:...) custom-call(bf16[1,640,768]{2,1,0:T(8,128)(2,1)} %bitcast.11, ...), custom_call_target="tpu_custom_call" | custom-call | tf_op jit(solution)/shard_map/deliver/pallas_call | solution.py:1308

commit v3 on v2

--- a/solution.py
+++ b/solution.py
@@ -523,9 +523,8 @@
             (3, lambda: gather_y(0)),
             (4, lambda: gather_z(2)),
             (6, lambda: gather_y(1)),
-            (7, lambda: gather_z(3)),
-            (8, lambda: gather_y(2)),
-            (10, lambda: gather_y(3)),
+            (8, lambda: gather_z(3)),
+            (9, lambda: gather_y(2)),
         ]
     project(me)
     x_copy(1).wait_recv()
@@ -536,6 +535,7 @@
     settle(me)
     context_r[at(me, group)] = context_s[me]
     if split:
+        gather_y(3)
         gather_end()
 
         def unpack(i, unused):
@@ -643,13 +643,23 @@
 
     run(n_steps, lambda i: (i,), expand, activate, raw0, raw1)
 
-    def contract(g, acc):
-        out = mm(wd[at(g, group)], act[at(g, hid)], 1, 0)
-        v = out + first[at(g, group)] + col(g, group, 5)
+    def clear_rows(count):
+        for n in range(count):
+            tops[n] = zero_row
+
+    part0, part1 = seed.at[0:group], seed.at[group : 2 * group]
+
+    def contract(raw, g):
+        raw[...] = mm(wd[at(g, group)], act[at(g, hid)], 1, 0)
+
+    def add_branch(raw, g):
+        v = raw[...] + first[at(g, group)] + col(g, group, 5)
         v2[at(g, group)] = v
-        return (acc + sub(v),)
-
-    (acc,) = loop(GROUPS, contract, zero_row)
+        tops[0] += sub(v)
+
+    clear_rows(1)
+    run(GROUPS, lambda g: (g,), contract, add_branch, part0, part1)
+    acc = tops[0]
     mean = acc * inv
     scale2 = center(v2)
 
@@ -685,24 +695,32 @@
 
     loop(GROUPS, back2, 0)
 
-    def back_act(i, unused):
+    raw0, raw1 = v2.at[0:span4], v2.at[span4 : 2 * span4]
+
+    def back_act(raw, i):
+        g, c = i // steps_group, lax.rem(i, steps_group)
+        raw[...] = mm(wd[at(g, group), at(c, span4)], low2[at(g, group)], 0, 0)
+
+    def times_slope(raw, i):
         place = at(i, span4)
-        g, c = i // steps_group, lax.rem(i, steps_group)
-        raw = mm(wd[at(g, group), at(c, span4)], low2[at(g, group)], 0, 0)
-        slope[place] = (raw * slope[place].astype(F32)).astype(BF16)
-        return (unused,)
-
-    loop(n_steps, back_act, 0)
-
-    def back_first(g, a, b):
+        slope[place] = (raw[...] * slope[place].astype(F32)).astype(BF16)
+
+    run(n_steps, lambda i: (i,), back_act, times_slope, raw0, raw1)
+    part0, part1 = v2.at[0:group], v2.at[group : 2 * group]
+
+    def back_first(raw, g):
+        raw[...] = mm(w_up[at(g, group)], slope[at(g, hid)], 1, 0)
+
+    def add_first(raw, g):
         place = at(g, group)
-        grad = seed[place] + mm(w_up[place], slope[at(g, hid)], 1, 0)
+        grad = seed[place] + raw[...]
         xhat = v1[place]
         vcols[place, 1:2] = jnp.sum(grad * xhat, axis=1, keepdims=True)
         vcols[place, 2:3] = jnp.sum(grad, axis=1, keepdims=True)
         grad = grad * col(g, group, 3)
         seed[place] = grad
-        return (a + sub(grad), b + sub(grad * xhat))
+        tops[0] += sub(grad)
+        tops[1] += sub(grad * xhat)
 
 
     vecs = r.vecs
@@ -842,8 +860,9 @@
                     pack[g * per_group + t, c, 1] = out[base : base + half].astype(BF16)
         else:
             r.g_all[1, g * group : (g + 1) * group] = out[0:group].astype(BF16)
-    sum1, sum2 = loop(GROUPS, back_first, zero_row, zero_row)
-    sum1, sum2 = sum1 * inv, sum2 * inv
+    clear_rows(2)
+    run(GROUPS, lambda g: (g,), back_first, add_first, part0, part1)
+    sum1, sum2 = tops[0] * inv, tops[1] * inv
 
     for g in range(GROUPS):
         out = mm(low2[g * group : (g + 1) * group], act[g * hid : (g + 1) * hid], 1, 1)

time: 152 us -> 148 us (0.974)
  Pallas kernels: 150 us -> 146 us
    pallas_call x1, Pallas kernels: 146 us -> 142 us  [layer(): pl.pallas_call(functools.partial(layer_kernel, cfg, row, names), out_shap...]
where the time goes in v3:
time: 148 us; the launch traced here: 147 us
  Pallas kernels  146 us (99%)
  between operations  1.5 us (1%)
    pallas_call x1, Pallas kernels, layer(): pl.pallas_call(functools.partial(layer_kernel, cfg, row, names), out_shap...  142 us
    pallas_call x1, Pallas kernels, deliver(): pl.pallas_call(functools.partial(deliver_kernel, cfg), out_shape=out_shap...  3.65 us

profile of v3, /device:TPU:0, one launch (start us, length us, event | category | flops | bytes accessed | tf_op | source)
XLA Modules:
  0.0 147.4 jit_solution(12623826625425363820)
XLA Ops:
  1.3 142.2 %layer.1 = (bf16[640,768]{1,0:T(8,128)(2,1)}, bf16[640,768]{1,0:T(8,128)(2,1)}, f32[2,3,48,768]{3,2,1,0:T(8,128)}, bf16[3,96,256]{2,1,0:T(8,128)(2,1)}, f32[16,768]{1,0:T(8,128)}) custom-call(bf16[640,768]{1,0:T(8,128)(2,1)} %bitcast.8, bf16[640,768]{1,0:T(8,128)(2,1)} %bitcast.9, bf16[640,768]{1,0:T(8,128)(2,1)} %bitcast.10, bf16[96,192]{1,0:T(8,128)(2,1)} %refs_3_.1, ...), custom_call_target="tpu_custom_call" | custom-call | tf_op jit(solution)/shard_map/layer/pallas_call | solution.py:1266
  143.5 3.6 %deliver.1 = (bf16[1,640,768]{2,1,0:T(8,128)(2,1)}, bf16[1,640,768]{2,1,0:T(8,128)(2,1)}, f32[96,192]{1,0:T(8,128)}, f32[96,192]{1,0:T(8,128)}, f32[96,192]{1,0:...) custom-call(bf16[1,640,768]{2,1,0:T(8,128)(2,1)} %bitcast.11, ...), custom_call_target="tpu_custom_call" | custom-call | tf_op jit(solution)/shard_map/deliver/pallas_call | solution.py:1327

commit v4 on v3

--- a/solution.py
+++ b/solution.py
@@ -19,7 +19,7 @@
 MESH = pl.DeviceIdType.MESH
 F32 = jnp.float32
 BF16 = jnp.bfloat16
-VMEM_LIMIT = 60 * 1024 * 1024
+VMEM_LIMIT = 61 * 1024 * 1024
 
 
 def mm(left, right, left_dim, right_dim):
@@ -574,13 +574,19 @@
 
     step = 256
 
-    def attn_out(i, acc):
-        out = mm(wo[:, at(i, step)], context_r[...], 0, 0)
-        v = out + x_own[at(i, step)].astype(F32) + col(i, step, 2)
+    raw0, raw1 = seed.at[0:step], seed.at[step : 2 * step]
+
+    def attn_out(raw, i):
+        raw[...] = mm(wo[:, at(i, step)], context_r[...], 0, 0)
+
+    def add_states(raw, i):
+        v = raw[...] + x_own[at(i, step)].astype(F32) + col(i, step, 2)
         v1[at(i, step)] = v
-        return (acc + sub(v),)
-
-    (acc,) = loop(width // step, attn_out, zero_row)
+        tops[0] += sub(v)
+
+    tops[0] = zero_row
+    run(width // step, lambda i: (i,), attn_out, add_states, raw0, raw1)
+    acc = tops[0]
     mean = acc * inv
 
     def center(ref):
@@ -802,7 +808,7 @@
                 copy.wait_recv()
 
             def add(i, unused):
-                side[i] = (pack[i, core].astype(F32) + side[i].astype(F32)).astype(BF16)
+                side[i] = pack[i, core] + side[i]
                 return (unused,)
 
             loop(n_dp, add, 0)
@@ -815,7 +821,7 @@
             cross_copy(j).wait_recv()
             z = lax.rem(my_z + 1 + j, n_z)
             i = 2 * z + my_y
-            side[i] = (side[i].astype(F32) + cross[z].astype(F32)).astype(BF16)
+            side[i] = side[i] + cross[z]
             if j < n_z - 1:
                 z_copy(j).start()
 
@@ -955,21 +961,15 @@
         dk[rows_of(h, k)] += mm(q_t[h, t, 0:HDIM], s[...], 1, 0)
         dq[rows_of(h, t)] += mm(k_t[h, k], s[...], 1, 1)
 
-    def turned(t, kind, h):
-        return pl.ds(pl.multiple_of((t * 3 + kind) * group + h * HDIM, HDIM), HDIM)
-
     def fill(t, h):
         for kind, (ref, scale) in enumerate(((dq, HDIM**-0.5), (dk, 1.0 / LOG2E), (dv, 1.0))):
-            d_t[turned(t, kind, h)] = (ref[rows_of(h, t)] * scale).astype(BF16)
-
-    def whole(t, kind):
-        return pl.ds(pl.multiple_of((t * 3 + kind) * group, HDIM), group)
+            place = pl.ds(pl.multiple_of(((t * heads + h) * 3 + kind) * HDIM, HDIM), HDIM)
+            d_t[place] = (ref[rows_of(h, t)] * scale).astype(BF16)
+
+    w_rows = r.w_rows
 
     def states_part(t):
-        out = mm(w_group[0], d_t[whole(t, 0)], 1, 0)
-        out += mm(w_group[1], d_t[whole(t, 1)], 1, 0)
-        out += mm(w_group[2], d_t[whole(t, 2)], 1, 0)
-        dx_s[at(t, group)] = out.astype(BF16)
+        dx_s[at(t, group)] = mm(w_rows[...], d_t[at(t, 3 * group)], 1, 0).astype(BF16)
 
     if split:
         qkv_s, qkv_r, qkv_out = r.qkv_s, r.qkv_r, r.qkv_out
@@ -992,25 +992,26 @@
     def emit(h):
         for d in range(2):
             fill(me ^ d, h)
-        totals = []
-        for kind in range(3):
-            value = mm(x_group[0], d_t[turned(0, kind, h)], 1, 1)
-            for t in range(1, seq):
-                value += mm(x_group[t], d_t[turned(t, kind, h)], 1, 1)
-            totals.append(value)
+        total = mm(x_group[0], d_t[at(h, 3 * HDIM)], 1, 1)
+        for t in range(1, seq):
+            total += mm(x_group[t], d_t[at(t * heads + h, 3 * HDIM)], 1, 1)
         if split:
             bias_rows = jnp.zeros((shard, HDIM), F32)
             bias_id = iota((shard, HDIM), 0)
             for kind in range(3):
-                bias_rows = jnp.where(bias_id == kind, totals[kind][group : group + 1], bias_rows)
+                bias_rows = jnp.where(
+                    bias_id == kind,
+                    total[group : group + 1, kind * HDIM : (kind + 1) * HDIM],
+                    bias_rows,
+                )
             for t in range(per_group):
                 qkv_s[h, t] = jnp.concatenate(
-                    [value[t * shard : (t + 1) * shard] for value in totals] + [bias_rows], axis=1
+                    [total[t * shard : (t + 1) * shard], bias_rows], axis=1
                 ).astype(BF16)
                 when(me * per_group + t != my_dp, lambda: qkv_copy(h, t).start())
         else:
             for kind in range(3):
-                r.qkv_raw[h, kind] = totals[kind]
+                r.qkv_raw[h, kind] = total[:, kind * HDIM : (kind + 1) * HDIM]
 
     early = 2 * (2 * heads + 2)
     shift = 2 * per_part - early
@@ -1068,6 +1069,14 @@
         ]
     d_in[me] = c_grad[at(me, group)]
     prepare(me)
+    w_rows[...] = jnp.concatenate(
+        [
+            w_group[kind, :, h * HDIM : (h + 1) * HDIM].astype(F32)
+            for h in range(heads)
+            for kind in range(3)
+        ],
+        axis=1,
+    ).astype(BF16)
     run(
         4 * per_part,
         place_backward,
@@ -1184,6 +1193,7 @@
         x_own=vm((w, l), BF16),
         x_group=vm((s, g + AUG, l), BF16),
         w_group=vm((3, g, g), BF16),
+        w_rows=vm((g, 3 * g), BF16),
         w_pad=vm((3, g + AUG, h * LANES), BF16),
         q_t=vm((h, s, LANES, l), BF16),
         k_n=vm((h, s, l, LANES), BF16),

time: 148 us -> 147 us (level)
  no operation moved by 1% of the time
where the time goes in v4:
time: 147 us
  Pallas kernels  145 us (99%)
  between operations  1.5 us (1%)
    pallas_call x1, Pallas kernels, layer(): pl.pallas_call(functools.partial(layer_kernel, cfg, row, names), out_shap...  142 us
    pallas_call x1, Pallas kernels, deliver(): pl.pallas_call(functools.partial(deliver_kernel, cfg), out_shape=out_shap...  3.65 us

profile of v4, /device:TPU:0, one launch (start us, length us, event | category | flops | bytes accessed | tf_op | source)
XLA Modules:
  0.0 146.7 jit_solution(15872551223982744273)
XLA Ops:
  1.3 141.5 %layer.1 = (bf16[640,768]{1,0:T(8,128)(2,1)}, bf16[640,768]{1,0:T(8,128)(2,1)}, f32[2,3,48,768]{3,2,1,0:T(8,128)}, bf16[3,96,256]{2,1,0:T(8,128)(2,1)}, f32[16,768]{1,0:T(8,128)}) custom-call(bf16[640,768]{1,0:T(8,128)(2,1)} %bitcast.8, bf16[640,768]{1,0:T(8,128)(2,1)} %bitcast.9, bf16[640,768]{1,0:T(8,128)(2,1)} %bitcast.10, bf16[96,192]{1,0:T(8,128)(2,1)} %refs_3_.1, ...), custom_call_target="tpu_custom_call" | custom-call | tf_op jit(solution)/shard_map/layer/pallas_call | solution.py:1276
  142.9 3.6 %deliver.1 = (bf16[1,640,768]{2,1,0:T(8,128)(2,1)}, bf16[1,640,768]{2,1,0:T(8,128)(2,1)}, f32[96,192]{1,0:T(8,128)}, f32[96,192]{1,0:T(8,128)}, f32[96,192]{1,0:...) custom-call(bf16[1,640,768]{2,1,0:T(8,128)(2,1)} %bitcast.11, ...), custom_call_target="tpu_custom_call" | custom-call | tf_op jit(solution)/shard_map/deliver/pallas_call | solution.py:1337

commit v5 on v4

--- a/solution.py
+++ b/solution.py
@@ -1287,12 +1287,17 @@
     return dict(zip(outputs, results, strict=True))
 
 
-def deliver_kernel(cfg, layer_in, states_in, qkv, od, vec, *refs):
-    outs = refs
+def deliver_kernel(cfg, layer_in, states_in, qkv, od, vec, *outs):
+    outs[0][...] = layer_in[...]
+    outs[1][...] = states_in[...]
+    pl.when((pl.program_id(0) == 0) & (pl.program_id(1) == 0))(
+        lambda: deliver_rest(cfg, qkv, od, vec, outs)
+    )
+
+
+def deliver_rest(cfg, qkv, od, vec, outs):
     my_dp = lax.axis_index("dp")
     shard, width, half = cfg.shard, cfg.width, cfg.half
-    outs[0][...] = layer_in[...]
-    outs[1][...] = states_in[...]
     qw, kw, vw, ow, uw, dw = outs[2:8]
     parts = [
         jnp.concatenate(
@@ -1333,12 +1338,21 @@
     out_shape += [sds((shard, group), F32)] * 3 + [sds((shard, width), F32)] * 2
     out_shape += [sds((group, 4 * shard), F32)] + [sds((shard,), F32)] * 8
     out_shape += [sds((4 * shard,), F32), sds((1,), F32)]
-    vmem = pl.BlockSpec(memory_space=pltpu.VMEM)
+    rows, slots, _ = args[0].shape
+    step = slots // 2 if slots % 32 == 0 else slots
+    tiles = pl.BlockSpec((1, step, width), lambda i, j: (i, j, 0))
+
+    def whole(a):
+        return pl.BlockSpec(a.shape, lambda i, j: (0,) * len(a.shape))
+
     return pl.pallas_call(
         functools.partial(deliver_kernel, cfg),
         out_shape=out_shape,
-        in_specs=[vmem] * len(args),
-        out_specs=[vmem] * (len(out_shape) - 1) + [pl.BlockSpec(memory_space=pltpu.SMEM)],
+        grid=(rows, slots // step),
+        in_specs=[tiles] * 2 + [whole(a) for a in args[2:]],
+        out_specs=[tiles] * 2
+        + [whole(a) for a in out_shape[2:-1]]
+        + [pl.BlockSpec((1,), lambda i, j: (0,), memory_space=pltpu.SMEM)],
         name="deliver",
     )(*args)
 

time: 147 us -> 147 us (level)
  no operation moved by 1% of the time
where the time goes in v5:
time: 147 us
  Pallas kernels  145 us (99%)
  between operations  1.5 us (1%)
    pallas_call x1, Pallas kernels, layer(): pl.pallas_call(functools.partial(layer_kernel, cfg, row, names), out_shap...  142 us
    pallas_call x1, Pallas kernels, deliver(): pl.pallas_call(functools.partial(deliver_kernel, cfg), out_shape=out_shap...  3.53 us

profile of v5, /device:TPU:0, one launch (start us, length us, event | category | flops | bytes accessed | tf_op | source)
XLA Modules:
  0.0 146.6 jit_solution(14484782236160987403)
XLA Ops:
  1.3 141.5 %layer.1 = (bf16[640,768]{1,0:T(8,128)(2,1)}, bf16[640,768]{1,0:T(8,128)(2,1)}, f32[2,3,48,768]{3,2,1,0:T(8,128)}, bf16[3,96,256]{2,1,0:T(8,128)(2,1)}, f32[16,768]{1,0:T(8,128)}) custom-call(bf16[640,768]{1,0:T(8,128)(2,1)} %bitcast.8, bf16[640,768]{1,0:T(8,128)(2,1)} %bitcast.9, bf16[640,768]{1,0:T(8,128)(2,1)} %bitcast.10, bf16[96,192]{1,0:T(8,128)(2,1)} %refs_3_.1, ...), custom_call_target="tpu_custom_call" | custom-call | tf_op jit(solution)/shard_map/layer/pallas_call | solution.py:1276
  142.9 3.5 %deliver.1 = (bf16[1,640,768]{2,1,0:T(8,128)(2,1)}, bf16[1,640,768]{2,1,0:T(8,128)(2,1)}, f32[96,192]{1,0:T(8,128)}, f32[96,192]{1,0:T(8,128)}, f32[96,192]{1,0:...) custom-call(bf16[1,640,768]{2,1,0:T(8,128)(2,1)} %bitcast.11, ...), custom_call_target="tpu_custom_call" | custom-call | tf_op jit(solution)/shard_map/deliver/pallas_call | solution.py:1348
